TPU v7x, 512 devices: a whole 4x8x8 slice. The times are simulated.
512 devices in a mesh: dp: 64 (over y, x, core), head: 8 (over z).
Axes of the slice: x: 4, y: 8, z: 8, core: 2. Of those that a mesh axis runs over, the one named last changes fastest.
Arguments:
- q_in: bfloat16 [65536, 3072], P(('dp', 'head')), may hold values from -8 to 8
- k_in: bfloat16 [65536, 512], P(('dp', 'head')), may hold values from -8 to 8
- v_in: bfloat16 [65536, 512], P(('dp', 'head')), may hold values from -6 to 6
- dout: bfloat16 [65536, 3072], P(('dp', 'head')), may hold values from -6 to 6
- swap_plan: int32 [3, 512], P(None, ('dp', 'head')), may hold values from 0 to 1
- doc_ids: int32 [64, 8], P('dp'), may hold values from 0 to 2, never falling along the last dimension, each value on 1 to 5 neighbouring positions
Outputs:
- out: bfloat16 [65536, 3072], P(('dp', 'head'))
- dq: bfloat16 [65536, 3072], P(('dp', 'head'))
- dk: bfloat16 [65536, 512], P(('dp', 'head'))
- dv: bfloat16 [65536, 512], P(('dp', 'head'))
Inputs may be any that keep to these rules, and one draw needn't show every extreme that they name: `doc_ids`: each row never falls; every id 0 .. 2 appears in every row.
All inputs are finite; a program needn't handle non-finite values.
Results may differ from a plain program's by a relative error of at most 0.024.
Values may be sent and summed in bfloat16 or wider, within the bound.
A program may use at most 64 MiB of HBM per device.

v0:
```python
import jax
import jax.numpy as jnp
from jax import lax
from jax.sharding import PartitionSpec as P

HEAD_DIM = 128
TILE_ROWS = 128
ROUNDS = 3


def swapped(value, axis, apart):
    mask = 2**apart
    pairs = [(source, source ^ mask) for source in range(lax.axis_size(axis))]
    return lax.ppermute(value, axis, pairs)


def head_group(query, keys, values, grad_out, query_pos, query_doc, key_pos, key_doc):
    q_rows = query.shape[0]
    per_kv = query.shape[1]
    block = min(q_rows, 512)
    blocks = q_rows // block
    scale = HEAD_DIM ** (-0.5)

    def one_block(carry, pieces):
        q_block, g_block, pos_block, doc_block = pieces
        scores = (
            jnp.einsum("bgd,kd->gbk", q_block, keys, preferred_element_type=jnp.float32) * scale
        )
        allowed = (doc_block[:, None] == key_doc[None, :]) & (
            key_pos[None, :] <= pos_block[:, None]
        )
        scores = jnp.where(allowed[None], scores, -jnp.inf)
        peak = jnp.max(scores, axis=-1, keepdims=True)
        total = jnp.sum(jnp.exp(scores - peak), axis=-1, keepdims=True)
        probs = jnp.exp(scores - (peak + jnp.log(total)))
        weights = probs.astype(jnp.bfloat16)
        out_block = jnp.einsum(
            "gbk,kd->bgd", weights, values, preferred_element_type=jnp.float32
        ).astype(jnp.bfloat16)
        delta = jnp.sum(g_block.astype(jnp.float32) * out_block.astype(jnp.float32), axis=-1)
        dprobs = jnp.einsum("bgd,kd->gbk", g_block, values, preferred_element_type=jnp.float32)
        dscores = (probs * (dprobs - jnp.transpose(delta)[..., None]) * scale).astype(jnp.bfloat16)
        dq_block = jnp.einsum(
            "gbk,kd->bgd", dscores, keys, preferred_element_type=jnp.float32
        ).astype(jnp.bfloat16)
        dk_block = jnp.einsum("gbk,bgd->kd", dscores, q_block, preferred_element_type=jnp.float32)
        dv_block = jnp.einsum("gbk,bgd->kd", weights, g_block, preferred_element_type=jnp.float32)
        return ((carry[0] + dk_block, carry[1] + dv_block), (out_block, dq_block))

    zeros_kv = jnp.zeros((keys.shape[0], HEAD_DIM), jnp.float32)
    pieces = (
        query.reshape(blocks, block, per_kv, HEAD_DIM),
        grad_out.reshape(blocks, block, per_kv, HEAD_DIM),
        query_pos.reshape(blocks, block),
        query_doc.reshape(blocks, block),
    )
    (grad_keys, grad_values), (outs, grads) = lax.scan(one_block, (zeros_kv, zeros_kv), pieces)
    return (
        outs.reshape(q_rows, per_kv * HEAD_DIM),
        grads.reshape(q_rows, per_kv * HEAD_DIM),
        grad_keys,
        grad_values,
    )


def attend(query, keys, values, grad_out, query_pos, query_doc, key_pos, key_doc, kv_count):
    q_rows = query.shape[0]
    k_rows = keys.shape[0]
    per_kv = query.shape[1] // (HEAD_DIM * kv_count)
    query_split = query.reshape(q_rows, kv_count, per_kv, HEAD_DIM)
    grad_split = grad_out.reshape(q_rows, kv_count, per_kv, HEAD_DIM)
    key_split = keys.reshape(k_rows, kv_count, HEAD_DIM)
    value_split = values.reshape(k_rows, kv_count, HEAD_DIM)

    def per_head(head_index):

        def select_head(array):
            return lax.dynamic_index_in_dim(array, head_index, 1, keepdims=False)

        return head_group(
            select_head(query_split),
            select_head(key_split),
            select_head(value_split),
            select_head(grad_split),
            query_pos,
            query_doc,
            key_pos,
            key_doc,
        )

    outs, grads, grad_keys, grad_values = lax.map(per_head, jnp.arange(kv_count))

    def rejoin(array):
        return jnp.moveaxis(array, 0, 1).reshape(array.shape[1], -1)

    return (rejoin(outs), rejoin(grads), rejoin(grad_keys), rejoin(grad_values))


def on_device(q_in, k_in, v_in, dout, swap_plan, doc_ids):
    row_count = q_in.shape[0]
    q_width = q_in.shape[1]
    kv_width = k_in.shape[1]
    tile_count = row_count // TILE_ROWS
    kv_total = kv_width // HEAD_DIM
    head_devices = lax.axis_size("head")
    top_bit = lax.axis_size("dp").bit_length() - 1
    packed = jnp.concatenate([q_in, k_in, v_in], axis=1).reshape(tile_count, TILE_ROWS, -1)
    for turn_index in range(ROUNDS):
        others = swapped(packed, "dp", top_bit - 1 - turn_index)
        packed = jnp.where((swap_plan[turn_index] == 1)[:, None, None], others, packed)
    packed = packed.reshape(row_count, -1)
    query = packed[:, :q_width]
    keys = packed[:, q_width : q_width + kv_width]
    values = packed[:, q_width + kv_width :]
    group_length = row_count * head_devices
    key_pos = jnp.arange(group_length, dtype=jnp.int32)
    key_doc = jnp.repeat(doc_ids[0], TILE_ROWS)
    kv_local = max(1, kv_total // head_devices)
    head_query, head_grad = (
        lax.all_to_all(query, "head", split_axis=1, concat_axis=0, tiled=True),
        lax.all_to_all(dout, "head", split_axis=1, concat_axis=0, tiled=True),
    )
    copies_each = head_devices // kv_total

    def widen(array):
        shaped = array.reshape(row_count, kv_total, 1, HEAD_DIM)
        return jnp.repeat(shaped, copies_each, axis=2).reshape(row_count, head_devices * HEAD_DIM)

    keys_send, values_send = (widen(keys), widen(values))
    head_keys, head_values = (
        lax.all_to_all(keys_send, "head", split_axis=1, concat_axis=0, tiled=True),
        lax.all_to_all(values_send, "head", split_axis=1, concat_axis=0, tiled=True),
    )
    outs, grad_query, grad_keys, grad_values = attend(
        head_query, head_keys, head_values, head_grad, key_pos, key_doc, key_pos, key_doc, kv_local
    )
    out_rows, dq_rows = (
        lax.all_to_all(outs, "head", split_axis=0, concat_axis=1, tiled=True),
        lax.all_to_all(grad_query, "head", split_axis=0, concat_axis=1, tiled=True),
    )
    dk_parts, dv_parts = (
        lax.all_to_all(grad_keys, "head", split_axis=0, concat_axis=1, tiled=True),
        lax.all_to_all(grad_values, "head", split_axis=0, concat_axis=1, tiled=True),
    )
    copies_each = head_devices // kv_total
    dk_sum = jnp.sum(dk_parts.reshape(row_count, kv_total, copies_each, HEAD_DIM), axis=2)
    dv_sum = jnp.sum(dv_parts.reshape(row_count, kv_total, copies_each, HEAD_DIM), axis=2)
    dk_rows = dk_sum.reshape(row_count, kv_width).astype(jnp.bfloat16)
    dv_rows = dv_sum.reshape(row_count, kv_width).astype(jnp.bfloat16)
    grads_packed = jnp.concatenate([dq_rows, dk_rows, dv_rows], axis=1).reshape(
        tile_count, TILE_ROWS, -1
    )
    for turn_index in reversed(range(ROUNDS)):
        others = swapped(grads_packed, "dp", top_bit - 1 - turn_index)
        grads_packed = jnp.where((swap_plan[turn_index] == 1)[:, None, None], others, grads_packed)
    grads_packed = grads_packed.reshape(row_count, -1)
    dq_out = grads_packed[:, :q_width]
    dk_out = grads_packed[:, q_width : q_width + kv_width]
    dv_out = grads_packed[:, q_width + kv_width :]
    return (out_rows, dq_out, dk_out, dv_out)


def solution(mesh):
    return jax.shard_map(
        on_device,
        mesh=mesh,
        in_specs=(
            P(("dp", "head"), None),
            P(("dp", "head"), None),
            P(("dp", "head"), None),
            P(("dp", "head"), None),
            P(None, ("dp", "head")),
            P("dp", None),
        ),
        out_specs=(
            P(("dp", "head"), None),
            P(("dp", "head"), None),
            P(("dp", "head"), None),
            P(("dp", "head"), None),
        ),
        check_vma=False,
    )
```

profile of v0, /device:TPU:1, one launch (start us, length us, event | category | flops | bytes accessed | tf_op | source)
XLA Modules:
  0.0 428.8 jit_solution(9724085419088308428)
XLA Ops:
  0.6 1.6 copy.74
  2.2 1.0 copy.75
  3.3 1.0 copy.76
  4.4 8.3 %collective-permute-start = (bf16[1,128,4096]{1,2,0:T(8,128)(2,1)S(1)}, bf16[1,128,4096]{1,2,0:T(8,128)(2,1)S(1)}, u32[]{:S(2)}, u32[]{:S(2)}) collective-permute-start(bf16[1,128,4096]{1,2,0:T(8,128)(2,1)S(1)} %maximum_bitcast_fusion), channel_id=1, source_target_pairs={{0,256},{8,264},{16,272},{24,280},{32,288},{40,296},{48,304},{56,3... | collective-permute-start | bytes 3145736 | tf_op jit(solution)/shard_map/ppermute | solution.py:14
  12.7 1.4 fusion.37
  14.7 31.9 %collective-permute-done = bf16[1,128,4096]{1,2,0:T(8,128)(2,1)S(1)} collective-permute-done((bf16[1,128,4096]{1,2,0:T(8,128)(2,1)S(1)}, bf16[1,128,4096]{1,2,0:T(8,128)(2,1)S(1)}, u32[]{:S(2)}, u32[]{:S(2)}) %collective-permute-start) | collective-permute-done | bytes 1048608 | tf_op jit(solution)/shard_map/ppermute | solution.py:14
  46.8 16.2 %collective-permute-start.1 = (bf16[1,128,4096]{1,2,0:T(8,128)(2,1)S(1)}, bf16[1,128,4096]{1,2,0:T(8,128)(2,1)S(1)}, u32[]{:S(2)}, u32[]{:S(2)}) collective-permute-start(bf16[1,128,4096]{1,2,0:T(8,128)(2,1)S(1)} %broadcast_select_fusion), channel_id=1, source_target_pairs={{0,128},{8,136},{16,144},{24,152},{32,160},{40,168},{48,176},{56,1... | collective-permute-start | bytes 3145736 | tf_op jit(solution)/shard_map/ppermute | solution.py:14
  63.7 45.4 %collective-permute-done.1 = bf16[1,128,4096]{1,2,0:T(8,128)(2,1)S(1)} collective-permute-done((bf16[1,128,4096]{1,2,0:T(8,128)(2,1)S(1)}, bf16[1,128,4096]{1,2,0:T(8,128)(2,1)S(1)}, u32[]{:S(2)}, u32[]{:S(2)}) %collective-permute-start.1) | collective-permute-done | bytes 1048608 | tf_op jit(solution)/shard_map/ppermute | solution.py:14
  109.2 1.9 collective-permute-start.2
  111.1 1.2 copy.79
  112.3 10.0 %all-to-all-start.2 = ((bf16[128,8,384]{0,2,1:T(8,128)(2,1)}), bf16[128,8,384]{0,2,1:T(8,128)(2,1)S(1)}, u32[]{:S(2)}, u32[]{:S(2)}) async-start(bf16[128,8,384]{0,2,1:T(8,128)(2,1)} %bitcast.11), calls=%async_computation.2 | async-start | bytes 1572864 | tf_op jit(solution)/shard_map/all_to_all | solution.py:121
  123.0 12.3 %collective-permute-done.2 = bf16[1,128,4096]{1,2,0:T(8,128)(2,1)S(1)} collective-permute-done((bf16[1,128,4096]{1,2,0:T(8,128)(2,1)S(1)}, bf16[1,128,4096]{1,2,0:T(8,128)(2,1)S(1)}, u32[]{:S(2)}, u32[]{:S(2)}) %collective-permute-start.2) | collective-permute-done | bytes 1048608 | tf_op jit(solution)/shard_map/ppermute | solution.py:14
  135.3 1.0 copy-done.2
  136.4 9.5 %all-to-all-done.2 = bf16[128,8,384]{0,2,1:T(8,128)(2,1)S(1)} async-done(((bf16[128,8,384]{0,2,1:T(8,128)(2,1)}), bf16[128,8,384]{0,2,1:T(8,128)(2,1)S(1)}, u32[]{:S(2)}, u32[]{:S(2)}) %all-to-all-start.2) | async-done | bytes 786464 | tf_op jit(solution)/shard_map/all_to_all | solution.py:121
  146.6 3.4 all-to-all-start.3
  150.1 0.9 slice.39
  151.0 11.1 %all-to-all-done.3 = bf16[128,8,128]{0,2,1:T(8,128)(2,1)S(1)} async-done(((bf16[128,8,128]{0,2,1:T(8,128)(2,1)}), bf16[128,8,128]{0,2,1:T(8,128)(2,1)S(1)}, u32[]{:S(2)}, u32[]{:S(2)}) %all-to-all-start.3) | async-done | bytes 262176 | tf_op jit(solution)/shard_map/all_to_all | solution.py:132
  162.1 3.5 all-to-all-start
  165.8 21.5 %all-to-all-done = bf16[128,8,384]{0,2,1:T(8,128)(2,1)S(1)} async-done(((bf16[128,8,384]{0,2,1:T(8,128)(2,1)}), bf16[128,8,384]{0,2,1:T(8,128)(2,1)S(1)}, u32[]{:S(2)}, u32[]{:S(2)}) %all-to-all-start) | async-done | bytes 786464 | tf_op jit(solution)/shard_map/all_to_all | solution.py:120
  188.0 3.4 all-to-all-start.1
  192.8 1.4 copy.80
  194.2 2.0 reshape.212
  196.2 1.8 copy.83
  198.2 0.9 copy.84
  199.6 1.2 reshape.210
  200.8 2.3 copy.82
  203.1 44.4 %while.30 = (s32[]{:T(128)}, f32[1024,128]{1,0:T(8,128)S(1)}, f32[1024,128]{1,0:T(8,128)}, bf16[2,512,3,128]{3,1,2,0:T(8,128)(2,1)}, bf16[2,512,3,128]{3,1,2,0:T...) while((s32[]{:T(128)}, f32[1024,128]{1,0:T(8,128)S(1)}, ...), condition=%wide.region_4.5_spmd.clone, body=%wide.region_0.4_spmd.clone.sunk | while | flops 2453795840 | bytes 116879776 | solution.py:57
  204.0 1.4 bitcast_reduce_fusion.4
  205.4 2.7 copy-done
  208.0 1.8 fusion.63
  209.9 5.6 %fusion.66 = f32[1024,128]{1,0:T(8,128)} fusion(f32[1024,128]{1,0:T(8,128)} %get-tuple-element.353, bf16[2,512,3,128]{3,1,2,0:T(8,128)(2,1)S(1)} %copy-done.4, s32[]{:T(128)} %get-tuple-element.351, pred[]{:T(512)S(6)} %compare.3, f32[512,3,1024]{2,0,1:T(8,128)} %copy-done, f32[3,512]{1,0:T(4,128)S(1)} %log_add_fusion.2, ...), kind=kOutput, calls=%fused_computation.21.clone.1 | convolution fusion | flops 409206784 | bytes 8265733 | tf_op jit(solution)/shard_map/while/body/eval_jaxpr/while/body/eval_jaxpr/gbk,bgd->kd/dot_general | solution.py:47
  215.5 3.1 multiply_reduce_fusion.2
  218.6 3.5 fusion.64
  222.1 1.1 fusion.67
  223.3 1.1 fusion.65
  224.5 0.9 copy-done.6
  226.1 1.4 bitcast_reduce_fusion.4
  227.4 2.7 copy-done
  230.1 1.8 fusion.63
  232.0 5.7 %fusion.66 = f32[1024,128]{1,0:T(8,128)} fusion(f32[1024,128]{1,0:T(8,128)} %get-tuple-element.353, bf16[2,512,3,128]{3,1,2,0:T(8,128)(2,1)S(1)} %copy-done.4, s32[]{:T(128)} %get-tuple-element.351, pred[]{:T(512)S(6)} %compare.3, f32[512,3,1024]{2,0,1:T(8,128)} %copy-done, f32[3,512]{1,0:T(4,128)S(1)} %log_add_fusion.2, ...), kind=kOutput, calls=%fused_computation.21.clone.1 | convolution fusion | flops 409206784 | bytes 8265733 | tf_op jit(solution)/shard_map/while/body/eval_jaxpr/while/body/eval_jaxpr/gbk,bgd->kd/dot_general | solution.py:47
  237.6 3.1 multiply_reduce_fusion.2
  240.7 3.5 fusion.64
  244.3 1.1 fusion.67
  245.4 1.1 fusion.65
  246.7 0.9 copy-done.6
  247.5 20.2 %all_to_all.134 = f32[8,128,128]{2,1,0:T(8,128)S(1)} all-to-all(f32[8,128,128]{2,1,0:T(8,128)S(1)} %bitcast.193), channel_id=1, replica_groups=mesh['dp'=64,'head'=8] {'head'}, dimensions={0} | all-to-all | bytes 1048576 | tf_op jit(solution)/shard_map/all_to_all | solution.py:142
  267.7 3.8 all-to-all-start.7
  271.5 2.3 copy.87
  274.4 1.0 copy.88
  275.4 9.1 %all-to-all-done.7 = f32[8,128,128]{2,1,0:T(8,128)S(1)} async-done(((f32[8,128,128]{2,1,0:T(8,128)}), f32[8,128,128]{2,1,0:T(8,128)S(1)}, u32[]{:S(2)}, u32[]{:S(2)}) %all-to-all-start.7) | async-done | bytes 524320 | tf_op jit(solution)/shard_map/all_to_all | solution.py:143
  284.4 3.5 all-to-all-start.5
  288.3 17.6 %all-to-all-done.5 = bf16[8,128,384]{1,2,0:T(8,128)(2,1)S(1)} async-done(((bf16[8,128,384]{1,2,0:T(8,128)(2,1)}), bf16[8,128,384]{1,2,0:T(8,128)(2,1)S(1)}, u32[]{:S(2)}, u32[]{:S(2)}) %all-to-all-start.5) | async-done | bytes 786464 | tf_op jit(solution)/shard_map/all_to_all | solution.py:139
  306.0 3.4 collective-permute-start.3
  309.4 17.1 %collective-permute-done.3 = bf16[1,128,4096]{1,2,0:T(8,128)(2,1)S(1)} collective-permute-done((bf16[1,128,4096]{1,2,0:T(8,128)(2,1)S(1)}, bf16[1,128,4096]{1,2,0:T(8,128)(2,1)S(1)}, u32[]{:S(2)}, u32[]{:S(2)}) %collective-permute-start.3) | collective-permute-done | bytes 1048608 | tf_op jit(solution)/shard_map/ppermute | solution.py:14
  326.8 1.9 collective-permute-start.4
  329.9 1.0 copy.86
  330.9 5.4 %all-to-all-start.4 = ((bf16[8,128,384]{1,2,0:T(8,128)(2,1)}), bf16[8,128,384]{1,2,0:T(8,128)(2,1)S(1)}, u32[]{:S(2)}, u32[]{:S(2)}) async-start(bf16[8,128,384]{1,2,0:T(8,128)(2,1)} %copy.86), calls=%async_computation.4 | async-start | bytes 1572864 | tf_op jit(solution)/shard_map/all_to_all | solution.py:138
  336.3 39.8 %collective-permute-done.4 = bf16[1,128,4096]{1,2,0:T(8,128)(2,1)} collective-permute-done((bf16[1,128,4096]{1,2,0:T(8,128)(2,1)S(1)}, bf16[1,128,4096]{1,2,0:T(8,128)(2,1)}, u32[]{:S(2)}, u32[]{:S(2)}) %collective-permute-start.4) | collective-permute-done | bytes 1048608 | tf_op jit(solution)/shard_map/ppermute | solution.py:14
  376.2 2.7 collective-permute-start.5
  378.9 1.2 copy.91
  380.1 45.8 %collective-permute-done.5 = bf16[1,128,4096]{1,2,0:T(8,128)(2,1)S(1)} collective-permute-done((bf16[1,128,4096]{1,2,0:T(8,128)(2,1)S(1)}, bf16[1,128,4096]{1,2,0:T(8,128)(2,1)S(1)}, u32[]{:S(2)}, u32[]{:S(2)}) %collective-permute-start.5) | collective-permute-done | bytes 1048608 | tf_op jit(solution)/shard_map/ppermute | solution.py:14
  426.1 1.2 copy.92
  427.2 0.8 copy.93
  428.0 0.8 copy.94
  (76 shorter events, 8.4 us)
Async XLA Ops:
  0.6 110.5 %copy-start.3 = (bf16[128,3072]{1,0:T(8,128)(2,1)S(1)}, bf16[128,3072]{1,0:T(8,128)(2,1)}, u32[]{:S(2)}) copy-start(bf16[128,3072]{1,0:T(8,128)(2,1)} %param.11) | copy-start | bytes 2359300
  4.4 42.2 %collective-permute-start = (bf16[1,128,4096]{1,2,0:T(8,128)(2,1)S(1)}, bf16[1,128,4096]{1,2,0:T(8,128)(2,1)S(1)}, u32[]{:S(2)}, u32[]{:S(2)}) collective-permute-start(bf16[1,128,4096]{1,2,0:T(8,128)(2,1)S(1)} %maximum_bitcast_fusion), channel_id=1, source_target_pairs={{0,256},{8,264},{16,272},{24,280},{32,288},{40,296},{48,304},{56,3... | collective-permute-start | bytes 3145736 | tf_op jit(solution)/shard_map/ppermute | solution.py:14
  46.8 62.2 %collective-permute-start.1 = (bf16[1,128,4096]{1,2,0:T(8,128)(2,1)S(1)}, bf16[1,128,4096]{1,2,0:T(8,128)(2,1)S(1)}, u32[]{:S(2)}, u32[]{:S(2)}) collective-permute-start(bf16[1,128,4096]{1,2,0:T(8,128)(2,1)S(1)} %broadcast_select_fusion), channel_id=1, source_target_pairs={{0,128},{8,136},{16,144},{24,152},{32,160},{40,168},{48,176},{56,1... | collective-permute-start | bytes 3145736 | tf_op jit(solution)/shard_map/ppermute | solution.py:14
  109.2 82.8 %copy-start.10 = (s32[1,8]{1,0:T(1,128)S(1)}, s32[1,8]{1,0:T(1,128)}, u32[]{:S(2)}) copy-start(s32[1,8]{1,0:T(1,128)} %param.13) | copy-start | bytes 100
  109.2 26.1 %collective-permute-start.2 = (bf16[1,128,4096]{1,2,0:T(8,128)(2,1)S(1)}, bf16[1,128,4096]{1,2,0:T(8,128)(2,1)S(1)}, u32[]{:S(2)}, u32[]{:S(2)}) collective-permute-start(bf16[1,128,4096]{1,2,0:T(8,128)(2,1)S(1)} %broadcast_select_fusion.2), channel_id=1, source_target_pairs={{0,64},{8,72},{16,80},{24,88},{32,96},{40,104},{48,112},{56,120},{... | collective-permute-start | bytes 3145736 | tf_op jit(solution)/shard_map/ppermute | solution.py:14
  112.3 33.6 %all-to-all-start.2 = ((bf16[128,8,384]{0,2,1:T(8,128)(2,1)}), bf16[128,8,384]{0,2,1:T(8,128)(2,1)S(1)}, u32[]{:S(2)}, u32[]{:S(2)}) async-start(bf16[128,8,384]{0,2,1:T(8,128)(2,1)} %bitcast.11), calls=%async_computation.2 | async-start | bytes 1572864 | tf_op jit(solution)/shard_map/all_to_all | solution.py:121
  135.3 1.0 copy-start.2
  146.6 15.4 %all-to-all-start.3 = ((bf16[128,8,128]{0,2,1:T(8,128)(2,1)}), bf16[128,8,128]{0,2,1:T(8,128)(2,1)S(1)}, u32[]{:S(2)}, u32[]{:S(2)}) async-start(bf16[128,8,128]{0,2,1:T(8,128)(2,1)} %bitcast.14), calls=%async_computation.3 | async-start | bytes 524288 | tf_op jit(solution)/shard_map/all_to_all | solution.py:132
  162.1 25.2 %all-to-all-start = ((bf16[128,8,384]{0,2,1:T(8,128)(2,1)}), bf16[128,8,384]{0,2,1:T(8,128)(2,1)S(1)}, u32[]{:S(2)}, u32[]{:S(2)}) async-start(bf16[128,8,384]{0,2,1:T(8,128)(2,1)} %bitcast.200), calls=%async_computation | async-start | bytes 1572864 | tf_op jit(solution)/shard_map/all_to_all | solution.py:120
  188.0 15.1 %all-to-all-start.1 = ((bf16[128,8,128]{2,0,1:T(8,128)(2,1)}), bf16[128,8,128]{2,0,1:T(8,128)(2,1)S(1)}, u32[]{:S(2)}, u32[]{:S(2)}) async-start(bf16[128,8,128]{2,0,1:T(8,128)(2,1)} %bitcast.8), calls=%async_computation.1 | async-start | bytes 524288 | tf_op jit(solution)/shard_map/all_to_all | solution.py:131
  204.0 5.9 %copy-start.4 = (bf16[2,512,3,128]{3,1,2,0:T(8,128)(2,1)S(1)}, bf16[2,512,3,128]{3,1,2,0:T(8,128)(2,1)}, u32[]{:S(2)}) copy-start(bf16[2,512,3,128]{3,1,2,0:T(8,128)(2,1)} %get-tuple-element.374) | copy-start | bytes 2359300 | tf_op jit(solution)/shard_map/while/body/eval_jaxpr/while
  205.4 2.7 copy-start
  209.9 5.6 %copy-start.1 = (f32[512,3,1024]{2,0,1:T(8,128)S(1)}, f32[512,3,1024]{2,0,1:T(8,128)}, u32[]{:S(2)}) copy-start(f32[512,3,1024]{2,0,1:T(8,128)} %copy-done) | copy-start | bytes 18874372 | tf_op jit(solution)/shard_map/while/body/eval_jaxpr/while
  218.5 3.6 copy-start.8
  222.1 2.3 copy-start.5
  223.3 1.2 copy-start.9
  224.5 0.9 copy-start.6
  226.1 5.9 %copy-start.4 = (bf16[2,512,3,128]{3,1,2,0:T(8,128)(2,1)S(1)}, bf16[2,512,3,128]{3,1,2,0:T(8,128)(2,1)}, u32[]{:S(2)}) copy-start(bf16[2,512,3,128]{3,1,2,0:T(8,128)(2,1)} %get-tuple-element.374) | copy-start | bytes 2359300 | tf_op jit(solution)/shard_map/while/body/eval_jaxpr/while
  227.4 2.7 copy-start
  231.9 5.7 %copy-start.1 = (f32[512,3,1024]{2,0,1:T(8,128)S(1)}, f32[512,3,1024]{2,0,1:T(8,128)}, u32[]{:S(2)}) copy-start(f32[512,3,1024]{2,0,1:T(8,128)} %copy-done) | copy-start | bytes 18874372 | tf_op jit(solution)/shard_map/while/body/eval_jaxpr/while
  240.7 3.6 copy-start.8
  244.2 2.3 copy-start.5
  245.4 1.2 copy-start.9
  246.6 0.9 copy-start.6
  267.7 16.7 %all-to-all-start.7 = ((f32[8,128,128]{2,1,0:T(8,128)}), f32[8,128,128]{2,1,0:T(8,128)S(1)}, u32[]{:S(2)}, u32[]{:S(2)}) async-start(f32[8,128,128]{2,1,0:T(8,128)} %bitcast.26), calls=%async_computation.7 | async-start | bytes 1048576 | tf_op jit(solution)/shard_map/all_to_all | solution.py:143
  273.8 54.9 %copy-start.7 = (bf16[2,512,3,128]{3,1,2,0:T(8,128)(2,1)S(1)}, bf16[2,512,3,128]{3,1,2,0:T(8,128)(2,1)}, u32[]{:S(2)}) copy-start(bf16[2,512,3,128]{3,1,2,0:T(8,128)(2,1)} %get-tuple-element.107) | copy-start | bytes 2359300
  284.4 21.5 %all-to-all-start.5 = ((bf16[8,128,384]{1,2,0:T(8,128)(2,1)}), bf16[8,128,384]{1,2,0:T(8,128)(2,1)S(1)}, u32[]{:S(2)}, u32[]{:S(2)}) async-start(bf16[8,128,384]{1,2,0:T(8,128)(2,1)} %copy.88), calls=%async_computation.5 | async-start | bytes 1572864 | tf_op jit(solution)/shard_map/all_to_all | solution.py:139
  306.0 20.5 %collective-permute-start.3 = (bf16[1,128,4096]{1,2,0:T(8,128)(2,1)S(1)}, bf16[1,128,4096]{1,2,0:T(8,128)(2,1)S(1)}, u32[]{:S(2)}, u32[]{:S(2)}) collective-permute-start(bf16[1,128,4096]{1,2,0:T(8,128)(2,1)S(1)} %maximum_bitcast_fusion.1), channel_id=1, source_target_pairs={{0,64},{8,72},{16,80},{24,88},{32,96},{40,104},{48,112},{56,120},{... | collective-permute-start | bytes 3145736 | tf_op jit(solution)/shard_map/ppermute | solution.py:14
  326.8 49.3 %collective-permute-start.4 = (bf16[1,128,4096]{1,2,0:T(8,128)(2,1)S(1)}, bf16[1,128,4096]{1,2,0:T(8,128)(2,1)}, u32[]{:S(2)}, u32[]{:S(2)}) collective-permute-start(bf16[1,128,4096]{1,2,0:T(8,128)(2,1)S(1)} %broadcast_select_fusion.3), channel_id=1, source_target_pairs={{0,128},{8,136},{16,144},{24,152},{32,160},{40,168},{48,176},{56,1... | collective-permute-start | bytes 3145736 | tf_op jit(solution)/shard_map/ppermute | solution.py:14
  330.9 48.0 %all-to-all-start.4 = ((bf16[8,128,384]{1,2,0:T(8,128)(2,1)}), bf16[8,128,384]{1,2,0:T(8,128)(2,1)S(1)}, u32[]{:S(2)}, u32[]{:S(2)}) async-start(bf16[8,128,384]{1,2,0:T(8,128)(2,1)} %copy.86), calls=%async_computation.4 | async-start | bytes 1572864 | tf_op jit(solution)/shard_map/all_to_all | solution.py:138
  376.2 49.7 %collective-permute-start.5 = (bf16[1,128,4096]{1,2,0:T(8,128)(2,1)S(1)}, bf16[1,128,4096]{1,2,0:T(8,128)(2,1)S(1)}, u32[]{:S(2)}, u32[]{:S(2)}) collective-permute-start(bf16[1,128,4096]{1,2,0:T(8,128)(2,1)S(1)} %broadcast_select_fusion.1), channel_id=1, source_target_pairs={{0,256},{8,264},{16,272},{24,280},{32,288},{40,296},{48,304},{56,3... | collective-permute-start | bytes 3145736 | tf_op jit(solution)/shard_map/ppermute | solution.py:14
where the time goes:
time: 432 us; the launch traced here: 429 us
  waiting for transfers between devices  261 us (60%)
  starting transfers between devices  67.5 us (16%)
  local copies, waits for them, and re-layouts  38.2 us (9%)
  matrix products  31.7 us (7%)
  blocking collectives  20.2 us (5%)
  other arithmetic  6.65 us (2%)
    ppermute x6, waiting for transfers between devices, swapped(): return lax.ppermute(value, axis, pairs)  192 us
    ppermute x6, starting transfers between devices, swapped(): return lax.ppermute(value, axis, pairs)  34.4 us
    all_to_all x1, waiting for transfers between devices, on_device(): lax.all_to_all(query, 'head', split_axis=1, concat_axis=0, tiled=True)  21.5 us
    all_to_all x1, blocking collectives, on_device(): lax.all_to_all(grad_keys, 'head', split_axis=0, concat_axis=1, tiled=True)  20.2 us
    all_to_all x1, waiting for transfers between devices, on_device(): lax.all_to_all(grad_query, 'head', split_axis=0, concat_axis=1, tiled=True)  17.6 us
    unnamed x22, local copies, waits for them, and re-layouts  15.2 us
    dot_general x2, matrix products, one_block(): jnp.einsum('gbk,bgd->kd', weights, g_block, preferred_element_type=jnp.fl...  11.2 us
    all_to_all x1, waiting for transfers between devices, on_device(): lax.all_to_all(values_send, 'head', split_axis=1, concat_axis=0, tiled=True)  11.1 us
  transfers between devices with their start and end apart: 13, of which 11 were waited for; matrix products, arithmetic and copies ran while one was open for 5% of the time, Pallas kernels for 0%

commit v1 on v0

v1 whole, which is shorter than its diff:
```python
import functools

import jax
import jax.numpy as jnp
from jax import lax
from jax.experimental import pallas as pl
from jax.experimental.pallas import tpu as pltpu
from jax.sharding import PartitionSpec as P

HD = 128
TILE = 128
NY = 8
NX = 4
NZ = 8
NH = 3
SLOTS = 5
SCALE = HD**-0.5
LOG2E = 1.4426950408889634
FAR = -1e30
MESH = pl.DeviceIdType.MESH
F32 = jnp.float32
BF16 = jnp.bfloat16


def exchange(tiles, masks, rounds):
    tiles = list(tiles)
    for r in rounds:
        stride = 4 >> r
        tiles = [jnp.where(masks[r][y], tiles[y ^ stride], tiles[y]) for y in range(NY)]
    return tiles


def kernel(
    swap_ref, docs_ref, q_ref, k_ref, v_ref, g_ref,
    out_ref, dq_ref, dk_ref, dv_ref,
    meta_src, meta, kv_raw, kv, kv_t, q_raw, q_bal, g_in,
    o_buf, dq_bal, dq_buf, acc, pair_out, pair_in, chain_out, chain_in, fin,
    meta_ss, meta_rs, kv_ss, kv_rs, q_ss, q_rs, g_ss, g_rs,
    kz_ss, kz_rs, kc_ss, kc_rs, o_ss, o_rs, dq_ss, dq_rs,
    pc_ss, pc_rs, cz_ss, cz_rs, f_ss, f_rs,
):
    dp = lax.axis_index("dp")
    z = lax.axis_index("head")
    y, x, c = dp // (2 * NX), (dp // 2) % NX, dp % 2
    own, other = y % 2, 1 - c
    kv_head = y // 2
    mate = dp + 1 - 2 * c

    def dp_of(yy, cc):
        return (yy * NX + x) * 2 + cc

    def move(src, dst, send_sem, recv_sem, target, here):
        @pl.when(jnp.logical_not(here))
        def _():
            pltpu.make_async_remote_copy(
                src, dst, send_sem, recv_sem, device_id=(target, z), device_id_type=MESH
            ).start()

        @pl.when(here)
        def _():
            pltpu.make_async_copy(src, dst, recv_sem).start()

    def wait(ref, sem):
        pltpu.make_async_copy(ref, ref, sem).wait()

    def wait_sent(ref, sem):
        @pl.when(own == c)
        def _():
            wait(ref.at[0 : NY - 1], sem)

        @pl.when(own != c)
        def _():
            wait(ref, sem)

    mine = docs_ref[0, z]
    meta_src[0:1, :] = jnp.zeros((1, HD), F32)
    for t in range(1, SLOTS):
        same = (docs_ref[0, jnp.maximum(z - t, 0)] == mine) & (z >= t)
        meta_src[t : t + 1, :] = jnp.full((1, HD), jnp.where(same, 0.0, FAR), F32)
    for r in range(3):
        meta_src[SLOTS + r : SLOTS + r + 1, :] = jnp.full((1, HD), swap_ref[r, 0].astype(F32), F32)

    barrier = pltpu.get_barrier_semaphore()
    me = y * 2 + c
    for step in range(1, 16):
        peer = lax.rem(me + step, 16)
        pl.semaphore_signal(barrier, inc=1, device_id=(dp_of(peer // 2, peer % 2), z), device_id_type=MESH)

    @pl.when(z < NZ - 1)
    def _():
        pl.semaphore_signal(barrier, inc=1, device_id=(dp, z + 1), device_id_type=MESH)

    @pl.when(z > 0)
    def _():
        pl.semaphore_signal(barrier, inc=1, device_id=(dp, z - 1), device_id_type=MESH)

    @pl.when((z > 0) & (z < NZ - 1))
    def _():
        pl.semaphore_wait(barrier, 17)

    @pl.when((z == 0) | (z == NZ - 1))
    def _():
        pl.semaphore_wait(barrier, 16)

    dests = []
    for i in range(4):
        for j in range(2):
            head, core = lax.rem(kv_head + i, 4), lax.rem(c + j, 2)
            to = 2 * head + c
            dests.append((head, core, to, (to == y) & (core == c)))
    for head, core, to, here in dests:
        move(meta_src, meta.at[y], meta_ss, meta_rs, dp_of(to, core), here)
    for head, core, to, here in dests:
        cols = pl.ds(pl.multiple_of(head * HD, HD), HD)

        @pl.when(core == 0)
        def _():
            move(k_ref.at[:, cols], kv_raw.at[y], kv_ss, kv_rs, dp_of(to, core), here)

        @pl.when(core == 1)
        def _():
            move(v_ref.at[:, cols], kv_raw.at[y], kv_ss, kv_rs, dp_of(to, core), here)

    for h in range(NH):
        for src, dst, ss, rs in ((q_ref, q_raw, q_ss, q_rs), (g_ref, g_in, g_ss, g_rs)):
            for head, core, to, here in dests:
                cols = pl.ds(pl.multiple_of((6 * head + 3 * core + h) * HD, HD), HD)
                move(src.at[:, cols], dst.at[h, y], ss.at[h], rs.at[h], dp_of(to, core), here)

    for t in range(1, SLOTS):

        @pl.when(z < t)
        def _():
            kv[:, :, t] = jnp.zeros((2, NY, TILE, HD), BF16)

    @pl.when(z == NZ - 1)
    def _():
        chain_in[...] = jnp.zeros_like(chain_in)

    wait(meta, meta_rs)
    wait(kv_raw, kv_rs)

    def masks_of():
        return [[meta[y_, SLOTS + r : SLOTS + r + 1, :] > 0.5 for y_ in range(NY)] for r in range(3)]

    def place(read, write, rounds):
        masks = masks_of()

        def rows(i, carry):
            at = pl.ds(pl.multiple_of(i * 16, 16), 16)
            tiles = exchange([read(y_, at) for y_ in range(NY)], masks, rounds)
            for y_ in range(NY):
                write(y_, at, tiles[y_].astype(BF16))
            return carry

        lax.fori_loop(0, TILE // 16, rows, 0)

    def write_kv(y_, at, value):
        kv[c, y_, 0, at, :] = value

    place(lambda y_, at: kv_raw[y_, at, :].astype(F32), write_kv, (0, 1, 2))

    for t in range(SLOTS):
        if t > 0:

            @pl.when(z >= t)
            def _():
                wait(kv.at[0, :, t], kz_rs.at[t - 1])

        @pl.when(z >= t)
        def _():
            pltpu.make_async_remote_copy(
                kv.at[c, :, t], kv.at[c, :, t], kc_ss.at[t], kc_rs.at[t],
                device_id=(mate, z), device_id_type=MESH,
            ).start()

        if t < SLOTS - 1:

            @pl.when((z >= t) & (z < NZ - 1))
            def _():
                pltpu.make_async_remote_copy(
                    kv.at[c, :, t], kv.at[c, :, t + 1], kz_ss.at[t], kz_rs.at[t],
                    device_id=(dp, z + 1), device_id_type=MESH,
                ).start()

    for t in range(SLOTS):

        @pl.when(z >= t)
        def _():
            wait(kv.at[0, :, t], kc_rs.at[t])

    row = lax.broadcasted_iota(jnp.int32, (TILE, HD), 0)
    col = lax.broadcasted_iota(jnp.int32, (TILE, HD), 1)

    def attend(heads, first):
        lanes = len(heads) * TILE
        h0 = heads[0]

        def group(y_, carry):
            keys = kv[0, y_].reshape(SLOTS * TILE, HD)
            values = kv[1, y_].reshape(SLOTS * TILE, HD)
            if first:
                kv_t[0, y_] = keys.T
                kv_t[1, y_] = values.T
            query = q_bal[h0 : h0 + len(heads), y_].reshape(lanes, HD)
            grad = g_in[h0 : h0 + len(heads), y_].reshape(lanes, HD)
            nt = (((1,), (1,)), ((), ()))
            scores = lax.dot_general(keys, query, nt, preferred_element_type=F32) * (SCALE * LOG2E)
            parts = []
            for t in range(SLOTS):
                part = scores[t * TILE : (t + 1) * TILE]
                if t == 0:
                    causal = jnp.concatenate([row <= col] * len(heads), axis=1) if len(heads) > 1 else row <= col
                    part = jnp.where(causal, part, FAR)
                else:
                    bias = meta[y_, t : t + 1, :]
                    bias = jnp.concatenate([bias] * len(heads), axis=1) if len(heads) > 1 else bias
                    part = part + bias
                parts.append(part)
            scores = jnp.concatenate(parts, axis=0)
            peak = jnp.max(scores, axis=0, keepdims=True)
            probs = jnp.exp2(scores - peak)
            probs = probs * (1.0 / jnp.sum(probs, axis=0, keepdims=True))
            weights = probs.astype(BF16)
            out_t = jnp.dot(kv_t[1, y_], weights, preferred_element_type=F32)
            o_buf[h0 : h0 + len(heads), y_] = out_t.T.astype(BF16).reshape(len(heads), TILE, HD)
            dprobs = lax.dot_general(values, grad, nt, preferred_element_type=F32)
            delta = jnp.sum(probs * dprobs, axis=0, keepdims=True)
            dscores = (probs * (dprobs - delta)).astype(BF16)
            dq_t = jnp.dot(kv_t[0, y_], dscores, preferred_element_type=F32) * SCALE
            dq_bal[h0 : h0 + len(heads), y_] = dq_t.T.astype(BF16).reshape(len(heads), TILE, HD)
            dk = jnp.dot(dscores, query, preferred_element_type=F32).reshape(SLOTS, TILE, HD)
            dv = jnp.dot(weights, grad, preferred_element_type=F32).reshape(SLOTS, TILE, HD)
            if first:
                acc[0, y_] = dk
                acc[1, y_] = dv
            else:
                acc[0, y_] += dk
                acc[1, y_] += dv
            return carry

        for h in heads:
            wait(q_raw.at[h], q_rs.at[h])

            def write_q(y_, at, value, h=h):
                q_bal[h, y_, at, :] = value

            place(lambda y_, at, h=h: q_raw[h, y_, at, :].astype(F32), write_q, (0, 1, 2))
        for h in heads:
            wait(g_in.at[h], g_rs.at[h])
        lax.fori_loop(0, NY, group, 0)

        for h in heads:

            def write_dq(y_, at, value, h=h):
                dq_buf[h, y_, at, :] = value

            place(lambda y_, at, h=h: dq_bal[h, y_, at, :].astype(F32), write_dq, (2, 1, 0))
            cols = pl.ds(pl.multiple_of((6 * kv_head + 3 * c + h) * HD, HD), HD)
            for i in range(NY):
                to = lax.rem(y + i, NY)
                here = (to == y) & (own == c)
                move(o_buf.at[h, to], out_ref.at[:, cols], o_ss.at[h], o_rs, dp_of(to, own), here)
                move(dq_buf.at[h, to], dq_ref.at[:, cols], dq_ss.at[h], dq_rs, dp_of(to, own), here)

    attend((0, 1), True)
    attend((2,), False)

    for t in reversed(range(SLOTS)):

        @pl.when(z >= t)
        def _():
            pair_out[t] = acc[other, :, t].astype(BF16)
            pltpu.make_async_remote_copy(
                pair_out.at[t], pair_in.at[t], pc_ss.at[t], pc_rs.at[t],
                device_id=(mate, z), device_id_type=MESH,
            ).start()

    for t in reversed(range(1, SLOTS)):

        @pl.when(z >= t)
        def _():
            wait(pair_in.at[t], pc_rs.at[t])
            if t < SLOTS - 1:

                @pl.when(z < NZ - 1)
                def _():
                    wait(chain_in.at[t], cz_rs.at[t])

                chain_out[t - 1] = (acc[c, :, t] + pair_in[t].astype(F32) + chain_in[t].astype(F32)).astype(BF16)
            else:
                chain_out[t - 1] = (acc[c, :, t] + pair_in[t].astype(F32)).astype(BF16)
            pltpu.make_async_remote_copy(
                chain_out.at[t - 1], chain_in.at[t - 1], cz_ss.at[t - 1], cz_rs.at[t - 1],
                device_id=(dp, z - 1), device_id_type=MESH,
            ).start()

    wait(pair_in.at[0], pc_rs.at[0])

    @pl.when(z < NZ - 1)
    def _():
        wait(chain_in.at[0], cz_rs.at[0])

    factor = jnp.where(c == 0, SCALE, 1.0).astype(F32)

    def read_total(y_, at):
        total = acc[c, y_, 0, at, :] + pair_in[0, y_, at, :].astype(F32) + chain_in[0, y_, at, :].astype(F32)
        return total * factor

    def write_total(y_, at, value):
        fin[y_, at, :] = value

    place(read_total, write_total, (2, 1, 0))
    cols = pl.ds(pl.multiple_of(kv_head * HD, HD), HD)
    for i in range(NY):
        to = lax.rem(y + i, NY)
        here = (to == y) & (own == c)

        @pl.when(c == 0)
        def _():
            move(fin.at[to], dk_ref.at[:, cols], f_ss, f_rs.at[0], dp_of(to, own), here)

        @pl.when(c == 1)
        def _():
            move(fin.at[to], dv_ref.at[:, cols], f_ss, f_rs.at[1], dp_of(to, own), here)

    wait(out_ref, o_rs)
    wait(dq_ref, dq_rs)
    wait(dk_ref, f_rs.at[0])
    wait(dv_ref, f_rs.at[1])
    wait_sent(meta, meta_ss)
    wait_sent(kv_raw, kv_ss)
    wait_sent(fin, f_ss)
    for h in range(NH):
        wait_sent(q_raw.at[h], q_ss.at[h])
        wait_sent(g_in.at[h], g_ss.at[h])
        wait_sent(o_buf.at[h], o_ss.at[h])
        wait_sent(dq_buf.at[h], dq_ss.at[h])
    for t in range(SLOTS):

        @pl.when(z >= t)
        def _():
            wait(kv.at[0, :, t], kc_ss.at[t])
            wait(pair_out.at[t], pc_ss.at[t])

    for t in range(SLOTS - 1):

        @pl.when((z >= t) & (z < NZ - 1))
        def _():
            wait(kv.at[0, :, t], kz_ss.at[t])

        @pl.when(z >= t + 1)
        def _():
            wait(chain_out.at[t], cz_ss.at[t])


def on_device(q_in, k_in, v_in, dout, swap_plan, doc_ids):
    tile = (TILE, HD)
    dma = pltpu.SemaphoreType.DMA
    hbm, smem = pl.BlockSpec(memory_space=pl.ANY), pl.BlockSpec(memory_space=pltpu.SMEM)
    return pl.pallas_call(
        kernel,
        out_shape=[jax.ShapeDtypeStruct(a.shape, BF16) for a in (dout, q_in, k_in, v_in)],
        in_specs=[smem, smem, hbm, hbm, hbm, hbm],
        out_specs=[hbm] * 4,
        scratch_shapes=[
            pltpu.VMEM((8, HD), F32),
            pltpu.VMEM((NY, 8, HD), F32),
            pltpu.VMEM((NY, *tile), BF16),
            pltpu.VMEM((2, NY, SLOTS, *tile), BF16),
            pltpu.VMEM((2, NY, HD, SLOTS * TILE), BF16),
            pltpu.VMEM((NH, NY, *tile), BF16),
            pltpu.VMEM((NH, NY, *tile), BF16),
            pltpu.VMEM((NH, NY, *tile), BF16),
            pltpu.VMEM((NH, NY, *tile), BF16),
            pltpu.VMEM((NH, NY, *tile), BF16),
            pltpu.VMEM((NH, NY, *tile), BF16),
            pltpu.VMEM((2, NY, SLOTS, *tile), F32),
            pltpu.VMEM((SLOTS, NY, *tile), BF16),
            pltpu.VMEM((SLOTS, NY, *tile), BF16),
            pltpu.VMEM((SLOTS - 1, NY, *tile), BF16),
            pltpu.VMEM((SLOTS - 1, NY, *tile), BF16),
            pltpu.VMEM((NY, *tile), BF16),
            dma, dma, dma, dma,
            dma((NH,)), dma((NH,)), dma((NH,)), dma((NH,)),
            dma((SLOTS - 1,)), dma((SLOTS - 1,)), dma((SLOTS,)), dma((SLOTS,)),
            dma((NH,)), dma, dma((NH,)), dma,
            dma((SLOTS,)), dma((SLOTS,)), dma((SLOTS - 1,)), dma((SLOTS - 1,)),
            dma, dma((2,)),
        ],
        compiler_params=pltpu.CompilerParams(
            collective_id=0, has_side_effects=True, vmem_limit_bytes=48 << 20
        ),
    )(swap_plan, doc_ids, q_in, k_in, v_in, dout)


def solution(mesh):
    rows = P(("dp", "head"), None)
    return jax.shard_map(
        on_device,
        mesh=mesh,
        in_specs=(rows, rows, rows, rows, P(None, ("dp", "head")), P("dp", None)),
        out_specs=(rows, rows, rows, rows),
        check_vma=False,
    )
```

time: 432 us -> 115 us (0.27)
  the two profiles are of different devices: /device:TPU:1 before, /device:TPU:198 now
where the time goes in v1:
time: 115 us
  Pallas kernels  106 us (92%)
  local copies, waits for them, and re-layouts  7.9 us (7%)
    pallas_call x1, Pallas kernels, on_device(): pl.pallas_call(kernel, out_shape=[jax.ShapeDtypeStruct(a.shape, BF16) for...  106 us
    unnamed x15, local copies, waits for them, and re-layouts  7.9 us

profile of v1, /device:TPU:198, one launch (start us, length us, event | category | flops | bytes accessed | tf_op | source)
XLA Modules:
  0.0 115.0 jit_solution(11546006784302526954)
XLA Ops:
  0.6 0.0 copy-start.4
  0.6 0.7 copy.10.swap_ref
  1.4 0.0 copy-done.4
  1.4 0.0 copy-start
  1.4 1.1 copy-done
  2.5 0.0 copy-start.1
  2.5 1.1 copy-done.1
  3.7 0.0 copy-start.2
  3.7 0.9 copy-done.2
  4.6 0.0 copy-start.3
  4.6 0.9 copy-done.3
  5.5 106.4 %shard_map.93 = (bf16[128,3072]{1,0:T(8,128)(2,1)S(1)}, bf16[128,3072]{1,0:T(8,128)(2,1)S(1)}, bf16[128,512]{1,0:T(8,128)(2,1)S(1)}, bf16[128,512]{1,0:T(8,128)(2,1)S(1)}) custom-call(s32[3,1]{1,0:T(4,128)S(1)} %copy.10.swap_ref, s32[1,8]{1,0:T(1,128)S(1)} %copy-done.4, bf16[128,3072]{1,0:T(8,128)(2,1)S(1)} %copy-done, bf16[128,512]{1,0:T(8,128)(2,1)S(1)} %copy-done.2, ...), custom_call_target="tpu_custom_call" | custom-call | tf_op jit(solution)/shard_map/pallas_call | solution.py:361
  111.9 0.9 copy.15
  112.8 0.9 copy.16
  113.7 0.7 copy.17
  114.3 0.7 copy.18
Async XLA Ops:
  0.6 0.8 copy-start.4
  1.4 1.1 copy-start
  2.5 1.1 copy-start.1
  3.7 0.9 copy-start.2
  4.6 0.9 copy-start.3

commit v2 on v1

v2 whole, which is shorter than its diff:
```python
import functools

import jax
import jax.numpy as jnp
from jax import lax
from jax.experimental import pallas as pl
from jax.experimental.pallas import tpu as pltpu
from jax.sharding import PartitionSpec as P

HD = 128
TILE = 128
NY = 8
NX = 4
NZ = 8
NH = 3
HALF = NY // 2
SLOTS = 5
SCALE = HD**-0.5
LOG2E = 1.4426950408889634
FAR = -1e30
MESH = pl.DeviceIdType.MESH
UPFRONT = ((0, 1, 2), (), ())
F32 = jnp.float32
BF16 = jnp.bfloat16


ORDER = (4, 3, 5, 2, 6, 1, 7, 0)


def exchange(tiles, masks, rounds):
    tiles = list(tiles)
    for r in rounds:
        stride = 4 >> r
        tiles = [jnp.where(masks[r][y], tiles[y ^ stride], tiles[y]) for y in range(NY)]
    return tiles


def kernel(
    swap_ref, docs_ref, q_ref, k_ref, v_ref, g_ref,
    out_ref, dq_ref, dk_ref, dv_ref,
    meta_src, meta, kv_raw, kv, kv_t, q_raw, q_bal, g_in,
    o_buf, dq_bal, dq_buf, acc, pair_out, pair_in, chain_out, chain_in, fin,
    meta_ss, meta_rs, kv_ss, kv_rs, q_ss, q_rs, g_ss, g_rs,
    kz_ss, kz_rs, kc_ss, kc_rs, o_ss, o_rs, dq_ss, dq_rs,
    pc_ss, pc_rs, cz_ss, cz_rs, f_ss, f_rs,
):
    dp = lax.axis_index("dp")
    z = lax.axis_index("head")
    y, x, c = dp // (2 * NX), (dp // 2) % NX, dp % 2
    own, other = y % 2, 1 - c
    kv_head = y // 2
    mate = dp + 1 - 2 * c

    def dp_of(yy, cc):
        return (yy * NX + x) * 2 + cc

    def move(src, dst, send_sem, recv_sem, target, here):
        @pl.when(jnp.logical_not(here))
        def _():
            pltpu.make_async_remote_copy(
                src, dst, send_sem, recv_sem, device_id=(target, z), device_id_type=MESH
            ).start()

        @pl.when(here)
        def _():
            pltpu.make_async_copy(src, dst, recv_sem).start()

    def wait(ref, sem):
        pltpu.make_async_copy(ref, ref, sem).wait()

    def wait_sent(ref, sem):
        @pl.when(own == c)
        def _():
            wait(ref.at[0 : NY - 1], sem)

        @pl.when(own != c)
        def _():
            wait(ref, sem)

    mine = docs_ref[0, z]
    meta_src[0:1, :] = jnp.zeros((1, HD), F32)
    for t in range(1, SLOTS):
        same = (docs_ref[0, jnp.maximum(z - t, 0)] == mine) & (z >= t)
        meta_src[t : t + 1, :] = jnp.full((1, HD), jnp.where(same, 0.0, FAR), F32)
    for r in range(3):
        meta_src[SLOTS + r : SLOTS + r + 1, :] = jnp.full((1, HD), swap_ref[0, r].astype(F32), F32)

    barrier = pltpu.get_barrier_semaphore()
    me = y * 2 + c
    for step in range(1, 16):
        peer = lax.rem(me + step, 16)
        pl.semaphore_signal(barrier, inc=1, device_id=(dp_of(peer // 2, peer % 2), z), device_id_type=MESH)

    @pl.when(z < NZ - 1)
    def _():
        pl.semaphore_signal(barrier, inc=1, device_id=(dp, z + 1), device_id_type=MESH)

    @pl.when(z > 0)
    def _():
        pl.semaphore_signal(barrier, inc=1, device_id=(dp, z - 1), device_id_type=MESH)

    @pl.when((z > 0) & (z < NZ - 1))
    def _():
        pl.semaphore_wait(barrier, 17)

    @pl.when((z == 0) | (z == NZ - 1))
    def _():
        pl.semaphore_wait(barrier, 16)

    dests = []
    for i in (2, 1, 3, 0):
        for j in range(2):
            head, core = lax.rem(kv_head + i, 4), lax.rem(c + j, 2)
            to = 2 * head + c
            dests.append((head, core, to, (to == y) & (core == c)))
    for head, core, to, here in dests:
        move(meta_src, meta.at[y], meta_ss, meta_rs, dp_of(to, core), here)
    for head, core, to, here in dests:
        cols = pl.ds(pl.multiple_of(head * HD, HD), HD)

        @pl.when(core == 0)
        def _():
            move(k_ref.at[:, cols], kv_raw.at[y], kv_ss, kv_rs, dp_of(to, core), here)

        @pl.when(core == 1)
        def _():
            move(v_ref.at[:, cols], kv_raw.at[y], kv_ss, kv_rs, dp_of(to, core), here)

    def send_heads(h):
        for src, dst, ss, rs in ((q_ref, q_raw, q_ss, q_rs), (g_ref, g_in, g_ss, g_rs)):
            for head, core, to, here in dests:
                cols = pl.ds(pl.multiple_of((6 * head + 3 * core + h) * HD, HD), HD)
                move(src.at[:, cols], dst.at[h, y], ss.at[h], rs.at[h], dp_of(to, core), here)

    for h in UPFRONT[0]:
        send_heads(h)

    for t in range(1, SLOTS):

        @pl.when(z < t)
        def _():
            kv[:, :, t] = jnp.zeros((2, NY, TILE, HD), BF16)

    @pl.when(z == NZ - 1)
    def _():
        chain_in[...] = jnp.zeros_like(chain_in)

    wait(meta, meta_rs)
    wait(kv_raw, kv_rs)

    def masks_of():
        return [[meta[y_, SLOTS + r : SLOTS + r + 1, :] > 0.5 for y_ in range(NY)] for r in range(3)]

    def place(read, write, rounds):
        masks = masks_of()

        def rows(i, carry):
            at = pl.ds(pl.multiple_of(i * 16, 16), 16)
            tiles = exchange([read(y_, at) for y_ in range(NY)], masks, rounds)
            for y_ in range(NY):
                write(y_, at, tiles[y_].astype(BF16))
            return carry

        lax.fori_loop(0, TILE // 16, rows, 0)

    def write_kv(y_, at, value):
        kv[c, y_, 0, at, :] = value

    place(lambda y_, at: kv_raw[y_, at, :].astype(F32), write_kv, (0, 1, 2))

    halves = [pl.ds(half * HALF, HALF) for half in range(2)]
    for t in range(SLOTS):
        for half in range(2):
            tiles = halves[half]
            if t > 0:

                @pl.when(z >= t)
                def _():
                    wait(kv.at[0, tiles, t], kz_rs.at[t - 1, half])

            @pl.when(z >= t)
            def _():
                pltpu.make_async_remote_copy(
                    kv.at[c, tiles, t], kv.at[c, tiles, t], kc_ss.at[t, half], kc_rs.at[t, half],
                    device_id=(mate, z), device_id_type=MESH,
                ).start()

            if t < SLOTS - 1:

                @pl.when((z >= t) & (z < NZ - 1))
                def _():
                    pltpu.make_async_remote_copy(
                        kv.at[c, tiles, t], kv.at[c, tiles, t + 1], kz_ss.at[t, half], kz_rs.at[t, half],
                        device_id=(dp, z + 1), device_id_type=MESH,
                    ).start()

        if t in (0, 1):
            for h in UPFRONT[t + 1]:
                send_heads(h)

    for t in range(SLOTS):
        for half in range(2):

            @pl.when(z >= t)
            def _():
                wait(kv.at[0, halves[half], t], kc_rs.at[t, half])

    def attend(heads, first, last):
        n = len(heads)
        lanes = n * TILE
        h0, h1 = heads[0], heads[-1] + 1
        nt = (((1,), (1,)), ((), ()))
        row = lax.broadcasted_iota(jnp.int32, (TILE, lanes), 0)
        col = lax.rem(lax.broadcasted_iota(jnp.int32, (TILE, lanes), 1), TILE)

        def group(i, carry):
            step = (i + 1) // 2
            y_ = lax.rem(y + 2 * NY + (HALF - step) * (2 * lax.rem(i, 2) - 1), NY)
            keys = kv[0, y_].reshape(SLOTS * TILE, HD)
            values = kv[1, y_].reshape(SLOTS * TILE, HD)
            if first:
                kv_t[0, y_] = keys.T
                kv_t[1, y_] = values.T
            query = q_bal[h0:h1, y_].reshape(lanes, HD)
            grad = g_in[h0:h1, y_].reshape(lanes, HD)
            scores = lax.dot_general(keys, query, nt, preferred_element_type=F32)
            dprobs = lax.dot_general(values, grad, nt, preferred_element_type=F32)
            parts = [scores[t * TILE : (t + 1) * TILE] for t in range(SLOTS)]
            parts[0] = jnp.where(row <= col, parts[0], FAR)
            bias = [jnp.concatenate([meta[y_, t : t + 1, :]] * n, axis=1) for t in range(SLOTS)]
            peaks = [jnp.max(parts[t], axis=0, keepdims=True) + bias[t] for t in range(SLOTS)]
            peak = functools.reduce(jnp.maximum, peaks)
            parts = [jnp.exp2((parts[t] - (peak - bias[t])) * (SCALE * LOG2E)) for t in range(SLOTS)]
            total = functools.reduce(jnp.add, [jnp.sum(part, axis=0, keepdims=True) for part in parts])
            inverse = 1.0 / total
            probs = jnp.concatenate([part * inverse for part in parts], axis=0)
            weights = probs.astype(BF16)
            delta = jnp.sum(probs * dprobs, axis=0, keepdims=True)
            dscores = (probs * (dprobs - delta)).astype(BF16)
            out_t = jnp.dot(kv_t[1, y_], weights, preferred_element_type=F32)
            o_buf[h0:h1, y_] = out_t.T.astype(BF16).reshape(n, TILE, HD)
            dq_t = jnp.dot(kv_t[0, y_], dscores, preferred_element_type=F32) * SCALE
            dq_bal[h0:h1, y_] = dq_t.T.astype(BF16).reshape(n, TILE, HD)
            dk = jnp.dot(dscores, query, preferred_element_type=F32).reshape(SLOTS, TILE, HD)
            dv = jnp.dot(weights, grad, preferred_element_type=F32).reshape(SLOTS, TILE, HD)
            if first:
                acc[0, i] = dk
                acc[1, i] = dv
            else:
                acc[0, i] += dk
                acc[1, i] += dv
            here = (y_ == y) & (own == c)
            for h in heads:
                cols = pl.ds(pl.multiple_of((6 * kv_head + 3 * c + h) * HD, HD), HD)
                move(o_buf.at[h, y_], out_ref.at[:, cols], o_ss.at[h], o_rs, dp_of(y_, own), here)
            if last:
                pair_out[i] = acc[other, i].astype(BF16)
                half = i // HALF
                pltpu.make_async_remote_copy(
                    pair_out.at[i], pair_in.at[i], pc_ss.at[half], pc_rs.at[half],
                    device_id=(mate, z), device_id_type=MESH,
                ).start()
            return carry

        for h in heads:
            wait(q_raw.at[h], q_rs.at[h])

            def write_q(y_, at, value, h=h):
                q_bal[h, y_, at, :] = value

            place(lambda y_, at, h=h: q_raw[h, y_, at, :].astype(F32), write_q, (0, 1, 2))
        for h in heads:
            wait(g_in.at[h], g_rs.at[h])
        lax.fori_loop(0, NY - 2 if last else NY, group, 0, unroll=2)
        if last:
            chain_step(SLOTS - 1, 0)
            lax.fori_loop(NY - 2, NY, group, 0, unroll=2)

    def send_dq(heads):
        for h in heads:

            def write_dq(y_, at, value, h=h):
                dq_buf[h, y_, at, :] = value

            place(lambda y_, at, h=h: dq_bal[h, y_, at, :].astype(F32), write_dq, (2, 1, 0))
            cols = pl.ds(pl.multiple_of((6 * kv_head + 3 * c + h) * HD, HD), HD)
            for i in ORDER:
                to = lax.rem(y + i, NY)
                here = (to == y) & (own == c)
                move(dq_buf.at[h, to], dq_ref.at[:, cols], dq_ss.at[h], dq_rs, dp_of(to, own), here)

    attend((0, 1), True, False)
    send_dq((0, 1))

    def chain_step(t, half):
        tiles = halves[half]
        if t == SLOTS - 1:
            wait(pair_in.at[tiles], pc_rs.at[half])

        @pl.when(z >= t)
        def _():
            if t < SLOTS - 1:

                @pl.when(z < NZ - 1)
                def _():
                    wait(chain_in.at[t, tiles], cz_rs.at[t, half])

            total = acc[c, tiles, t] + pair_in[tiles, t].astype(F32)
            if t < SLOTS - 1:
                total = total + chain_in[t, tiles].astype(F32)
            chain_out[t - 1, tiles] = total.astype(BF16)
            pltpu.make_async_remote_copy(
                chain_out.at[t - 1, tiles], chain_in.at[t - 1, tiles],
                cz_ss.at[t - 1, half], cz_rs.at[t - 1, half],
                device_id=(dp, z - 1), device_id_type=MESH,
            ).start()

    attend((2,), False, True)
    chain_step(SLOTS - 1, 1)
    send_dq((2,))
    for t in reversed(range(1, SLOTS - 1)):
        for half in range(2):
            chain_step(t, half)


    @pl.when(z < NZ - 1)
    def _():
        for half in range(2):
            wait(chain_in.at[0, halves[half]], cz_rs.at[0, half])

    factor = jnp.where(c == 0, SCALE, 1.0).astype(F32)

    def read_total(y_, at):
        d = lax.rem(y_ - y + NY, NY)
        i = (d // HALF) * (2 * (d - HALF)) + (1 - d // HALF) * (NY - 1 - 2 * d)
        total = acc[c, i, 0, at, :] + pair_in[i, 0, at, :].astype(F32) + chain_in[0, i, at, :].astype(F32)
        return total * factor

    def write_total(y_, at, value):
        fin[y_, at, :] = value

    place(read_total, write_total, (2, 1, 0))
    cols = pl.ds(pl.multiple_of(kv_head * HD, HD), HD)
    for i in ORDER:
        to = lax.rem(y + i, NY)
        here = (to == y) & (own == c)

        @pl.when(c == 0)
        def _():
            move(fin.at[to], dk_ref.at[:, cols], f_ss, f_rs.at[0], dp_of(to, own), here)

        @pl.when(c == 1)
        def _():
            move(fin.at[to], dv_ref.at[:, cols], f_ss, f_rs.at[1], dp_of(to, own), here)

    wait(out_ref, o_rs)
    wait(dq_ref, dq_rs)
    wait(dk_ref, f_rs.at[0])
    wait(dv_ref, f_rs.at[1])
    wait_sent(meta, meta_ss)
    wait_sent(kv_raw, kv_ss)
    wait_sent(fin, f_ss)
    for h in range(NH):
        wait_sent(q_raw.at[h], q_ss.at[h])
        wait_sent(g_in.at[h], g_ss.at[h])
        wait_sent(o_buf.at[h], o_ss.at[h])
        wait_sent(dq_buf.at[h], dq_ss.at[h])
    for half in range(2):
        tiles = halves[half]
        wait(pair_out.at[tiles], pc_ss.at[half])
        for t in range(SLOTS):

            @pl.when(z >= t)
            def _():
                wait(kv.at[0, tiles, t], kc_ss.at[t, half])

        for t in range(SLOTS - 1):

            @pl.when((z >= t) & (z < NZ - 1))
            def _():
                wait(kv.at[0, tiles, t], kz_ss.at[t, half])

            @pl.when(z >= t + 1)
            def _():
                wait(chain_out.at[t, tiles], cz_ss.at[t, half])


PIECES = 1


def hand_over(*refs):
    ins, outs, bufs, (read_sems, write_sems) = refs[0:4], refs[4:8], refs[8:12], refs[12:]
    pieces = [(a, pl.ds(p * (TILE // PIECES), TILE // PIECES)) for p in range(PIECES) for a in range(4)]
    reads = [pltpu.make_async_copy(ins[a].at[r], bufs[a].at[r], read_sems.at[i]) for i, (a, r) in enumerate(pieces)]
    writes = [pltpu.make_async_copy(bufs[a].at[r], outs[a].at[r], write_sems.at[i]) for i, (a, r) in enumerate(pieces)]
    for copy in reads:
        copy.start()
    for read, write in zip(reads, writes):
        read.wait()
        write.start()
    for copy in writes:
        copy.wait()


def on_device(q_in, k_in, v_in, dout, swap_plan, doc_ids):
    tile = (TILE, HD)
    dma = pltpu.SemaphoreType.DMA
    hbm, smem = pl.BlockSpec(memory_space=pl.ANY), pl.BlockSpec(memory_space=pltpu.SMEM)
    results = pl.pallas_call(
        kernel,
        out_shape=[jax.ShapeDtypeStruct(a.shape, BF16) for a in (dout, q_in, k_in, v_in)],
        in_specs=[smem, smem, hbm, hbm, hbm, hbm],
        out_specs=[hbm] * 4,
        scratch_shapes=[
            pltpu.VMEM((8, HD), F32),
            pltpu.VMEM((NY, 8, HD), F32),
            pltpu.VMEM((NY, *tile), BF16),
            pltpu.VMEM((2, NY, SLOTS, *tile), BF16),
            pltpu.VMEM((2, NY, HD, SLOTS * TILE), BF16),
            pltpu.VMEM((NH, NY, *tile), BF16),
            pltpu.VMEM((NH, NY, *tile), BF16),
            pltpu.VMEM((NH, NY, *tile), BF16),
            pltpu.VMEM((NH, NY, *tile), BF16),
            pltpu.VMEM((NH, NY, *tile), BF16),
            pltpu.VMEM((NH, NY, *tile), BF16),
            pltpu.VMEM((2, NY, SLOTS, *tile), F32),
            pltpu.VMEM((NY, SLOTS, *tile), BF16),
            pltpu.VMEM((NY, SLOTS, *tile), BF16),
            pltpu.VMEM((SLOTS - 1, NY, *tile), BF16),
            pltpu.VMEM((SLOTS - 1, NY, *tile), BF16),
            pltpu.VMEM((NY, *tile), BF16),
            dma, dma, dma, dma,
            dma((NH,)), dma((NH,)), dma((NH,)), dma((NH,)),
            dma((SLOTS - 1, 2)), dma((SLOTS - 1, 2)), dma((SLOTS, 2)), dma((SLOTS, 2)),
            dma((NH,)), dma, dma((NH,)), dma,
            dma((2,)), dma((2,)), dma((SLOTS - 1, 2)), dma((SLOTS - 1, 2)),
            dma, dma((2,)),
        ],
        compiler_params=pltpu.CompilerParams(
            collective_id=0, has_side_effects=True, vmem_limit_bytes=63 << 20
        ),
    )(swap_plan.reshape(1, 3), doc_ids, q_in, k_in, v_in, dout)
    return pl.pallas_call(
        hand_over,
        out_shape=[jax.ShapeDtypeStruct(a.shape, BF16) for a in results],
        in_specs=[hbm] * 4,
        out_specs=[hbm] * 4,
        scratch_shapes=[pltpu.VMEM(a.shape, BF16) for a in results] + [dma((4 * PIECES,)), dma((4 * PIECES,))],
    )(*results)


def solution(mesh):
    rows = P(("dp", "head"), None)
    return jax.shard_map(
        on_device,
        mesh=mesh,
        in_specs=(rows, rows, rows, rows, P(None, ("dp", "head")), P("dp", None)),
        out_specs=(rows, rows, rows, rows),
        check_vma=False,
    )
```

time: 115 us -> 98.2 us (0.85)
  the two profiles are of different devices: /device:TPU:198 before, /device:TPU:1 now
where the time goes in v2:
time: 98.2 us; the launch traced here: 98.1 us
  Pallas kernels  97.4 us (99%)
    pallas_call x1, Pallas kernels, on_device(): pl.pallas_call(kernel, out_shape=[jax.ShapeDtypeStruct(a.shape, BF16) for...  95 us
    pallas_call x1, Pallas kernels, on_device(): pl.pallas_call(hand_over, out_shape=[jax.ShapeDtypeStruct(a.shape, BF16)...  2.42 us

profile of v2, /device:TPU:1, one launch (start us, length us, event | category | flops | bytes accessed | tf_op | source)
XLA Modules:
  0.0 98.1 jit_solution(16226071204175813663)
XLA Ops:
  0.6 95.0 %shard_map.93 = (bf16[128,3072]{1,0:T(8,128)(2,1)}, bf16[128,3072]{1,0:T(8,128)(2,1)}, bf16[128,512]{1,0:T(8,128)(2,1)}, bf16[128,512]{1,0:T(8,128)(2,1)}) custom-call(s32[1,3]{1,0:T(1,128)} %bitcast.1, s32[1,8]{1,0:T(1,128)} %docs_ref.1, bf16[128,3072]{1,0:T(8,128)(2,1)} %q_ref.1, bf16[128,512]{1,0:T(8,128)(2,1)} %k_ref.1, bf16[128,512]{1,0:T(8,128)(2,1)} %v_ref.1, ...), custom_call_target="tpu_custom_call" | custom-call | tf_op jit(solution)/shard_map/pallas_call | solution.py:409
  95.7 2.4 %shard_map.94 = (bf16[128,3072]{1,0:T(8,128)(2,1)}, bf16[128,3072]{1,0:T(8,128)(2,1)}, bf16[128,512]{1,0:T(8,128)(2,1)}, bf16[128,512]{1,0:T(8,128)(2,1)}) custom-call(bf16[128,3072]{1,0:T(8,128)(2,1)} %get-tuple-element.8.refs_0_, bf16[128,3072]{1,0:T(8,128)(2,1)} %get-tuple-element.9.refs_1_, bf16[128,512]{1,0:T(8,128)(2,1)} %get-tuple-element.10.refs_2_, ...), custom_call_target="tpu_custom_call" | custom-call | tf_op jit(solution)/shard_map/pallas_call | solution.py:443

commit v3 on v2

--- a/solution.py
+++ b/solution.py
@@ -14,6 +14,8 @@
 NZ = 8
 NH = 3
 HALF = NY // 2
+PARTS = 4
+PART = NY // PARTS
 SLOTS = 5
 SCALE = HD**-0.5
 LOG2E = 1.4426950408889634
@@ -77,6 +79,20 @@
         def _():
             wait(ref, sem)
 
+    barrier = pltpu.get_barrier_semaphore()
+    me = y * 2 + c
+    for step in range(1, 16):
+        peer = lax.rem(me + step, 16)
+        pl.semaphore_signal(barrier, inc=1, device_id=(dp_of(peer // 2, peer % 2), z), device_id_type=MESH)
+
+    @pl.when(z < NZ - 1)
+    def _():
+        pl.semaphore_signal(barrier, inc=1, device_id=(dp, z + 1), device_id_type=MESH)
+
+    @pl.when(z > 0)
+    def _():
+        pl.semaphore_signal(barrier, inc=1, device_id=(dp, z - 1), device_id_type=MESH)
+
     mine = docs_ref[0, z]
     meta_src[0:1, :] = jnp.zeros((1, HD), F32)
     for t in range(1, SLOTS):
@@ -85,19 +101,15 @@
     for r in range(3):
         meta_src[SLOTS + r : SLOTS + r + 1, :] = jnp.full((1, HD), swap_ref[0, r].astype(F32), F32)
 
-    barrier = pltpu.get_barrier_semaphore()
-    me = y * 2 + c
-    for step in range(1, 16):
-        peer = lax.rem(me + step, 16)
-        pl.semaphore_signal(barrier, inc=1, device_id=(dp_of(peer // 2, peer % 2), z), device_id_type=MESH)
-
-    @pl.when(z < NZ - 1)
-    def _():
-        pl.semaphore_signal(barrier, inc=1, device_id=(dp, z + 1), device_id_type=MESH)
-
-    @pl.when(z > 0)
-    def _():
-        pl.semaphore_signal(barrier, inc=1, device_id=(dp, z - 1), device_id_type=MESH)
+    for t in range(1, SLOTS):
+
+        @pl.when(z < t)
+        def _():
+            kv[:, :, t] = jnp.zeros((2, NY, TILE, HD), BF16)
+
+    @pl.when(z == NZ - 1)
+    def _():
+        chain_in[...] = jnp.zeros_like(chain_in)
 
     @pl.when((z > 0) & (z < NZ - 1))
     def _():
@@ -134,16 +146,6 @@
 
     for h in UPFRONT[0]:
         send_heads(h)
-
-    for t in range(1, SLOTS):
-
-        @pl.when(z < t)
-        def _():
-            kv[:, :, t] = jnp.zeros((2, NY, TILE, HD), BF16)
-
-    @pl.when(z == NZ - 1)
-    def _():
-        chain_in[...] = jnp.zeros_like(chain_in)
 
     wait(meta, meta_rs)
     wait(kv_raw, kv_rs)
@@ -255,9 +257,9 @@
                 move(o_buf.at[h, y_], out_ref.at[:, cols], o_ss.at[h], o_rs, dp_of(y_, own), here)
             if last:
                 pair_out[i] = acc[other, i].astype(BF16)
-                half = i // HALF
+                part = i // PART
                 pltpu.make_async_remote_copy(
-                    pair_out.at[i], pair_in.at[i], pc_ss.at[half], pc_rs.at[half],
+                    pair_out.at[i], pair_in.at[i], pc_ss.at[part], pc_rs.at[part],
                     device_id=(mate, z), device_id_type=MESH,
                 ).start()
             return carry
@@ -271,10 +273,21 @@
             place(lambda y_, at, h=h: q_raw[h, y_, at, :].astype(F32), write_q, (0, 1, 2))
         for h in heads:
             wait(g_in.at[h], g_rs.at[h])
-        lax.fori_loop(0, NY - 2 if last else NY, group, 0, unroll=2)
-        if last:
-            chain_step(SLOTS - 1, 0)
-            lax.fori_loop(NY - 2, NY, group, 0, unroll=2)
+        if not last:
+            lax.fori_loop(0, NY, group, 0, unroll=2)
+            return
+
+        def some(part, carry):
+            for i in range(PART):
+                group(part * PART + i, carry)
+
+            @pl.when(part > 0)
+            def _():
+                chain_step(SLOTS - 1, part - 1)
+
+            return carry
+
+        lax.fori_loop(0, PARTS, some, 0)
 
     def send_dq(heads):
         for h in heads:
@@ -292,10 +305,10 @@
     attend((0, 1), True, False)
     send_dq((0, 1))
 
-    def chain_step(t, half):
-        tiles = halves[half]
+    def chain_step(t, part):
+        tiles = pl.ds(part * PART, PART)
         if t == SLOTS - 1:
-            wait(pair_in.at[tiles], pc_rs.at[half])
+            wait(pair_in.at[tiles], pc_rs.at[part])
 
         @pl.when(z >= t)
         def _():
@@ -303,7 +316,7 @@
 
                 @pl.when(z < NZ - 1)
                 def _():
-                    wait(chain_in.at[t, tiles], cz_rs.at[t, half])
+                    wait(chain_in.at[t, tiles], cz_rs.at[t, part])
 
             total = acc[c, tiles, t] + pair_in[tiles, t].astype(F32)
             if t < SLOTS - 1:
@@ -311,22 +324,26 @@
             chain_out[t - 1, tiles] = total.astype(BF16)
             pltpu.make_async_remote_copy(
                 chain_out.at[t - 1, tiles], chain_in.at[t - 1, tiles],
-                cz_ss.at[t - 1, half], cz_rs.at[t - 1, half],
+                cz_ss.at[t - 1, part], cz_rs.at[t - 1, part],
                 device_id=(dp, z - 1), device_id_type=MESH,
             ).start()
 
     attend((2,), False, True)
-    chain_step(SLOTS - 1, 1)
+    chain_step(SLOTS - 1, PARTS - 1)
     send_dq((2,))
     for t in reversed(range(1, SLOTS - 1)):
-        for half in range(2):
-            chain_step(t, half)
+
+        def step(part, carry, t=t):
+            chain_step(t, part)
+            return carry
+
+        lax.fori_loop(0, PARTS, step, 0)
 
 
     @pl.when(z < NZ - 1)
     def _():
-        for half in range(2):
-            wait(chain_in.at[0, halves[half]], cz_rs.at[0, half])
+        for part in range(PARTS):
+            wait(chain_in.at[0, part * PART : (part + 1) * PART], cz_rs.at[0, part])
 
     factor = jnp.where(c == 0, SCALE, 1.0).astype(F32)
 
@@ -367,7 +384,6 @@
         wait_sent(dq_buf.at[h], dq_ss.at[h])
     for half in range(2):
         tiles = halves[half]
-        wait(pair_out.at[tiles], pc_ss.at[half])
         for t in range(SLOTS):
 
             @pl.when(z >= t)
@@ -380,25 +396,21 @@
             def _():
                 wait(kv.at[0, tiles, t], kz_ss.at[t, half])
 
+    for part in range(PARTS):
+        tiles = pl.ds(part * PART, PART)
+        wait(pair_out.at[tiles], pc_ss.at[part])
+        for t in range(SLOTS - 1):
+
             @pl.when(z >= t + 1)
             def _():
-                wait(chain_out.at[t, tiles], cz_ss.at[t, half])
-
-
-PIECES = 1
+                wait(chain_out.at[t, tiles], cz_ss.at[t, part])
 
 
 def hand_over(*refs):
-    ins, outs, bufs, (read_sems, write_sems) = refs[0:4], refs[4:8], refs[8:12], refs[12:]
-    pieces = [(a, pl.ds(p * (TILE // PIECES), TILE // PIECES)) for p in range(PIECES) for a in range(4)]
-    reads = [pltpu.make_async_copy(ins[a].at[r], bufs[a].at[r], read_sems.at[i]) for i, (a, r) in enumerate(pieces)]
-    writes = [pltpu.make_async_copy(bufs[a].at[r], outs[a].at[r], write_sems.at[i]) for i, (a, r) in enumerate(pieces)]
-    for copy in reads:
+    copies = [pltpu.make_async_copy(refs[i], refs[4 + i], refs[8].at[i]) for i in range(4)]
+    for copy in copies:
         copy.start()
-    for read, write in zip(reads, writes):
-        read.wait()
-        write.start()
-    for copy in writes:
+    for copy in copies:
         copy.wait()
 
 
@@ -408,7 +420,7 @@
     hbm, smem = pl.BlockSpec(memory_space=pl.ANY), pl.BlockSpec(memory_space=pltpu.SMEM)
     results = pl.pallas_call(
         kernel,
-        out_shape=[jax.ShapeDtypeStruct(a.shape, BF16) for a in (dout, q_in, k_in, v_in)],
+        out_shape=[pltpu.VMEM(a.shape, BF16) for a in (dout, q_in, k_in, v_in)],
         in_specs=[smem, smem, hbm, hbm, hbm, hbm],
         out_specs=[hbm] * 4,
         scratch_shapes=[
@@ -433,20 +445,21 @@
             dma((NH,)), dma((NH,)), dma((NH,)), dma((NH,)),
             dma((SLOTS - 1, 2)), dma((SLOTS - 1, 2)), dma((SLOTS, 2)), dma((SLOTS, 2)),
             dma((NH,)), dma, dma((NH,)), dma,
-            dma((2,)), dma((2,)), dma((SLOTS - 1, 2)), dma((SLOTS - 1, 2)),
+            dma((PARTS,)), dma((PARTS,)), dma((SLOTS - 1, PARTS)), dma((SLOTS - 1, PARTS)),
             dma, dma((2,)),
         ],
         compiler_params=pltpu.CompilerParams(
-            collective_id=0, has_side_effects=True, vmem_limit_bytes=63 << 20
+            collective_id=0, has_side_effects=True, vmem_limit_bytes=62 << 20
         ),
     )(swap_plan.reshape(1, 3), doc_ids, q_in, k_in, v_in, dout)
     return pl.pallas_call(
         hand_over,
         out_shape=[jax.ShapeDtypeStruct(a.shape, BF16) for a in results],
-        in_specs=[hbm] * 4,
+        in_specs=[pl.BlockSpec(memory_space=pltpu.VMEM)] * 4,
         out_specs=[hbm] * 4,
-        scratch_shapes=[pltpu.VMEM(a.shape, BF16) for a in results] + [dma((4 * PIECES,)), dma((4 * PIECES,))],
-    )(*results)
+        scratch_shapes=[dma((4,))],
+        compiler_params=pltpu.CompilerParams(vmem_limit_bytes=1 << 20),
+    )(*[pltpu.with_memory_space_constraint(a, pltpu.VMEM) for a in results])
 
 
 def solution(mesh):

time: 98.2 us -> 95.3 us (0.970); the launches traced: 98.1 us -> 94.1 us
  Pallas kernels: 97.4 us -> 93.5 us
    pallas_call x1, Pallas kernels: 95 us -> 92.2 us  [on_device(): pl.pallas_call(kernel, out_shape=[pltpu.VMEM(a.shape, BF16) for a in (dou...]
    pallas_call x1, Pallas kernels: 2.42 us -> 1.25 us  [on_device(): pl.pallas_call(hand_over, out_shape=[jax.ShapeDtypeStruct(a.shape, BF16)...]
where the time goes in v3:
time: 95.3 us; the launch traced here: 94.1 us
  Pallas kernels  93.5 us (98%)
    pallas_call x1, Pallas kernels, on_device(): pl.pallas_call(kernel, out_shape=[pltpu.VMEM(a.shape, BF16) for a in (dou...  92.2 us

profile of v3, /device:TPU:1, one launch (start us, length us, event | category | flops | bytes accessed | tf_op | source)
XLA Modules:
  0.0 94.1 jit_solution(10982369498536502414)
XLA Ops:
  0.6 92.2 %shard_map.93 = (bf16[128,3072]{1,0:T(8,128)(2,1)S(1)}, bf16[128,3072]{1,0:T(8,128)(2,1)S(1)}, bf16[128,512]{1,0:T(8,128)(2,1)S(1)}, bf16[128,512]{1,0:T(8,128)(2,1)S(1)}) custom-call(s32[1,3]{1,0:T(1,128)} %bitcast.1, s32[1,8]{1,0:T(1,128)} %docs_ref.1, bf16[128,3072]{1,0:T(8,128)(2,1)} %q_ref.1, bf16[128,512]{1,0:T(8,128)(2,1)} %k_ref.1, ...), custom_call_target="tpu_custom_call" | custom-call | tf_op jit(solution)/shard_map/pallas_call | solution.py:421
  92.8 1.3 %shard_map.94 = (bf16[128,3072]{1,0:T(8,128)(2,1)}, bf16[128,3072]{1,0:T(8,128)(2,1)}, bf16[128,512]{1,0:T(8,128)(2,1)}, bf16[128,512]{1,0:T(8,128)(2,1)}) custom-call(bf16[128,3072]{1,0:T(8,128)(2,1)S(1)} %get-tuple-element.8.refs_0_, bf16[128,3072]{1,0:T(8,128)(2,1)S(1)} %get-tuple-element.9.refs_1_, bf16[128,512]{1,0:T(8,128)(2,1)S(1)} %get-tuple-element.10.refs_2_, ...), custom_call_target="tpu_custom_call" | custom-call | tf_op jit(solution)/shard_map/pallas_call | solution.py:455

commit v4 on v3

--- a/solution.py
+++ b/solution.py
@@ -16,6 +16,7 @@
 HALF = NY // 2
 PARTS = 4
 PART = NY // PARTS
+CUT = TILE // 2
 SLOTS = 5
 SCALE = HD**-0.5
 LOG2E = 1.4426950408889634
@@ -153,17 +154,17 @@
     def masks_of():
         return [[meta[y_, SLOTS + r : SLOTS + r + 1, :] > 0.5 for y_ in range(NY)] for r in range(3)]
 
-    def place(read, write, rounds):
+    def place(read, write, rounds, start=0, count=TILE):
         masks = masks_of()
 
         def rows(i, carry):
-            at = pl.ds(pl.multiple_of(i * 16, 16), 16)
+            at = pl.ds(pl.multiple_of(start + i * 16, 16), 16)
             tiles = exchange([read(y_, at) for y_ in range(NY)], masks, rounds)
             for y_ in range(NY):
                 write(y_, at, tiles[y_].astype(BF16))
             return carry
 
-        lax.fori_loop(0, TILE // 16, rows, 0)
+        lax.fori_loop(0, count // 16, rows, 0)
 
     def write_kv(y_, at, value):
         kv[c, y_, 0, at, :] = value
@@ -283,7 +284,7 @@
 
             @pl.when(part > 0)
             def _():
-                chain_step(SLOTS - 1, part - 1)
+                chain_begin(part - 1)
 
             return carry
 
@@ -305,10 +306,8 @@
     attend((0, 1), True, False)
     send_dq((0, 1))
 
-    def chain_step(t, part):
-        tiles = pl.ds(part * PART, PART)
-        if t == SLOTS - 1:
-            wait(pair_in.at[tiles], pc_rs.at[part])
+    def chain_step(t, part, cut):
+        tiles, rows = pl.ds(part * PART, PART), pl.ds(cut * CUT, CUT)
 
         @pl.when(z >= t)
         def _():
@@ -316,34 +315,36 @@
 
                 @pl.when(z < NZ - 1)
                 def _():
-                    wait(chain_in.at[t, tiles], cz_rs.at[t, part])
-
-            total = acc[c, tiles, t] + pair_in[tiles, t].astype(F32)
+                    wait(chain_in.at[t, tiles, rows], cz_rs.at[t, part, cut])
+
+            total = acc[c, tiles, t, rows] + pair_in[tiles, t, rows].astype(F32)
             if t < SLOTS - 1:
-                total = total + chain_in[t, tiles].astype(F32)
-            chain_out[t - 1, tiles] = total.astype(BF16)
+                total = total + chain_in[t, tiles, rows].astype(F32)
+            chain_out[t - 1, tiles, rows] = total.astype(BF16)
             pltpu.make_async_remote_copy(
-                chain_out.at[t - 1, tiles], chain_in.at[t - 1, tiles],
-                cz_ss.at[t - 1, part], cz_rs.at[t - 1, part],
+                chain_out.at[t - 1, tiles, rows], chain_in.at[t - 1, tiles, rows],
+                cz_ss.at[t - 1, part, cut], cz_rs.at[t - 1, part, cut],
                 device_id=(dp, z - 1), device_id_type=MESH,
             ).start()
 
+    def chain_begin(part):
+        wait(pair_in.at[pl.ds(part * PART, PART)], pc_rs.at[part])
+        for cut in range(2):
+            chain_step(SLOTS - 1, part, cut)
+
     attend((2,), False, True)
-    chain_step(SLOTS - 1, PARTS - 1)
+    chain_begin(PARTS - 1)
     send_dq((2,))
     for t in reversed(range(1, SLOTS - 1)):
 
-        def step(part, carry, t=t):
-            chain_step(t, part)
-            return carry
-
-        lax.fori_loop(0, PARTS, step, 0)
-
-
-    @pl.when(z < NZ - 1)
-    def _():
-        for part in range(PARTS):
-            wait(chain_in.at[0, part * PART : (part + 1) * PART], cz_rs.at[0, part])
+        for cut in range(2):
+
+            def step(part, carry, t=t, cut=cut):
+                chain_step(t, part, cut)
+                return carry
+
+            lax.fori_loop(0, PARTS, step, 0)
+
 
     factor = jnp.where(c == 0, SCALE, 1.0).astype(F32)
 
@@ -356,19 +357,27 @@
     def write_total(y_, at, value):
         fin[y_, at, :] = value
 
-    place(read_total, write_total, (2, 1, 0))
     cols = pl.ds(pl.multiple_of(kv_head * HD, HD), HD)
-    for i in ORDER:
-        to = lax.rem(y + i, NY)
-        here = (to == y) & (own == c)
-
-        @pl.when(c == 0)
-        def _():
-            move(fin.at[to], dk_ref.at[:, cols], f_ss, f_rs.at[0], dp_of(to, own), here)
-
-        @pl.when(c == 1)
-        def _():
-            move(fin.at[to], dv_ref.at[:, cols], f_ss, f_rs.at[1], dp_of(to, own), here)
+    for cut in range(2):
+        rows = pl.ds(cut * CUT, CUT)
+
+        @pl.when(z < NZ - 1)
+        def _():
+            for part in range(PARTS):
+                wait(chain_in.at[0, part * PART : (part + 1) * PART, rows], cz_rs.at[0, part, cut])
+
+        place(read_total, write_total, (2, 1, 0), cut * CUT, CUT)
+        for i in ORDER:
+            to = lax.rem(y + i, NY)
+            here = (to == y) & (own == c)
+
+            @pl.when(c == 0)
+            def _():
+                move(fin.at[to, rows], dk_ref.at[rows, cols], f_ss.at[cut], f_rs.at[0], dp_of(to, own), here)
+
+            @pl.when(c == 1)
+            def _():
+                move(fin.at[to, rows], dv_ref.at[rows, cols], f_ss.at[cut], f_rs.at[1], dp_of(to, own), here)
 
     wait(out_ref, o_rs)
     wait(dq_ref, dq_rs)
@@ -376,7 +385,8 @@
     wait(dv_ref, f_rs.at[1])
     wait_sent(meta, meta_ss)
     wait_sent(kv_raw, kv_ss)
-    wait_sent(fin, f_ss)
+    for cut in range(2):
+        wait_sent(fin.at[:, cut * CUT : (cut + 1) * CUT], f_ss.at[cut])
     for h in range(NH):
         wait_sent(q_raw.at[h], q_ss.at[h])
         wait_sent(g_in.at[h], g_ss.at[h])
@@ -403,7 +413,8 @@
 
             @pl.when(z >= t + 1)
             def _():
-                wait(chain_out.at[t, tiles], cz_ss.at[t, part])
+                for cut in range(2):
+                    wait(chain_out.at[t, tiles, cut * CUT : (cut + 1) * CUT], cz_ss.at[t, part, cut])
 
 
 def hand_over(*refs):
@@ -445,8 +456,8 @@
             dma((NH,)), dma((NH,)), dma((NH,)), dma((NH,)),
             dma((SLOTS - 1, 2)), dma((SLOTS - 1, 2)), dma((SLOTS, 2)), dma((SLOTS, 2)),
             dma((NH,)), dma, dma((NH,)), dma,
-            dma((PARTS,)), dma((PARTS,)), dma((SLOTS - 1, PARTS)), dma((SLOTS - 1, PARTS)),
-            dma, dma((2,)),
+            dma((PARTS,)), dma((PARTS,)), dma((SLOTS - 1, PARTS, 2)), dma((SLOTS - 1, PARTS, 2)),
+            dma((2,)), dma((2,)),
         ],
         compiler_params=pltpu.CompilerParams(
             collective_id=0, has_side_effects=True, vmem_limit_bytes=62 << 20

time: 95.3 us -> 95.5 us (level); the launches traced: 94.1 us -> 95.3 us
  Pallas kernels: 93.5 us -> 94.7 us
    pallas_call x1, Pallas kernels: 92.2 us -> 93.5 us  [on_device(): pl.pallas_call(kernel, out_shape=[pltpu.VMEM(a.shape, BF16) for a in (dou...]
where the time goes in v4:
time: 95.5 us; the launch traced here: 95.3 us
  Pallas kernels  94.7 us (99%)
    pallas_call x1, Pallas kernels, on_device(): pl.pallas_call(kernel, out_shape=[pltpu.VMEM(a.shape, BF16) for a in (dou...  93.5 us

profile of v4, /device:TPU:1, one launch (start us, length us, event | category | flops | bytes accessed | tf_op | source)
XLA Modules:
  0.0 95.3 jit_solution(12411145044587389505)
XLA Ops:
  0.6 93.5 %shard_map.93 = (bf16[128,3072]{1,0:T(8,128)(2,1)S(1)}, bf16[128,3072]{1,0:T(8,128)(2,1)S(1)}, bf16[128,512]{1,0:T(8,128)(2,1)S(1)}, bf16[128,512]{1,0:T(8,128)(2,1)S(1)}) custom-call(s32[1,3]{1,0:T(1,128)} %bitcast.1, s32[1,8]{1,0:T(1,128)} %docs_ref.1, bf16[128,3072]{1,0:T(8,128)(2,1)} %q_ref.1, bf16[128,512]{1,0:T(8,128)(2,1)} %k_ref.1, ...), custom_call_target="tpu_custom_call" | custom-call | tf_op jit(solution)/shard_map/pallas_call | solution.py:432
  94.1 1.3 %shard_map.94 = (bf16[128,3072]{1,0:T(8,128)(2,1)}, bf16[128,3072]{1,0:T(8,128)(2,1)}, bf16[128,512]{1,0:T(8,128)(2,1)}, bf16[128,512]{1,0:T(8,128)(2,1)}) custom-call(bf16[128,3072]{1,0:T(8,128)(2,1)S(1)} %get-tuple-element.8.refs_0_, bf16[128,3072]{1,0:T(8,128)(2,1)S(1)} %get-tuple-element.9.refs_1_, bf16[128,512]{1,0:T(8,128)(2,1)S(1)} %get-tuple-element.10.refs_2_, ...), custom_call_target="tpu_custom_call" | custom-call | tf_op jit(solution)/shard_map/pallas_call | solution.py:466

commit v5 on v4

--- a/solution.py
+++ b/solution.py
@@ -22,7 +22,6 @@
 LOG2E = 1.4426950408889634
 FAR = -1e30
 MESH = pl.DeviceIdType.MESH
-UPFRONT = ((0, 1, 2), (), ())
 F32 = jnp.float32
 BF16 = jnp.bfloat16
 
@@ -145,7 +144,7 @@
                 cols = pl.ds(pl.multiple_of((6 * head + 3 * core + h) * HD, HD), HD)
                 move(src.at[:, cols], dst.at[h, y], ss.at[h], rs.at[h], dp_of(to, core), here)
 
-    for h in UPFRONT[0]:
+    for h in range(NH):
         send_heads(h)
 
     wait(meta, meta_rs)
@@ -166,47 +165,39 @@
 
         lax.fori_loop(0, count // 16, rows, 0)
 
+    def turn(y_):
+        d = lax.rem(y_ - y + NY, NY)
+        return (d // HALF) * (2 * (d - HALF)) + (1 - d // HALF) * (NY - 1 - 2 * d)
+
     def write_kv(y_, at, value):
-        kv[c, y_, 0, at, :] = value
+        kv[c, turn(y_), 0, at, :] = value
 
     place(lambda y_, at: kv_raw[y_, at, :].astype(F32), write_kv, (0, 1, 2))
 
-    halves = [pl.ds(half * HALF, HALF) for half in range(2)]
-    for t in range(SLOTS):
-        for half in range(2):
-            tiles = halves[half]
+    def key_step(t, part):
+        tiles = pl.ds(part * PART, PART)
+
+        @pl.when(z >= t)
+        def _():
             if t > 0:
-
-                @pl.when(z >= t)
-                def _():
-                    wait(kv.at[0, tiles, t], kz_rs.at[t - 1, half])
-
-            @pl.when(z >= t)
+                wait(kv.at[0, tiles, t], kz_rs.at[t - 1, part])
+            pltpu.make_async_remote_copy(
+                kv.at[c, tiles, t], kv.at[c, tiles, t], kc_ss.at[t, part], kc_rs.at[t, part],
+                device_id=(mate, z), device_id_type=MESH,
+            ).start()
+
+        if t < SLOTS - 1:
+
+            @pl.when((z >= t) & (z < NZ - 1))
             def _():
                 pltpu.make_async_remote_copy(
-                    kv.at[c, tiles, t], kv.at[c, tiles, t], kc_ss.at[t, half], kc_rs.at[t, half],
-                    device_id=(mate, z), device_id_type=MESH,
+                    kv.at[c, tiles, t], kv.at[c, tiles, t + 1], kz_ss.at[t, part], kz_rs.at[t, part],
+                    device_id=(dp, z + 1), device_id_type=MESH,
                 ).start()
 
-            if t < SLOTS - 1:
-
-                @pl.when((z >= t) & (z < NZ - 1))
-                def _():
-                    pltpu.make_async_remote_copy(
-                        kv.at[c, tiles, t], kv.at[c, tiles, t + 1], kz_ss.at[t, half], kz_rs.at[t, half],
-                        device_id=(dp, z + 1), device_id_type=MESH,
-                    ).start()
-
-        if t in (0, 1):
-            for h in UPFRONT[t + 1]:
-                send_heads(h)
-
-    for t in range(SLOTS):
-        for half in range(2):
-
-            @pl.when(z >= t)
-            def _():
-                wait(kv.at[0, halves[half], t], kc_rs.at[t, half])
+    for t in range(SLOTS - 1):
+        for part in range(PARTS):
+            key_step(t, part)
 
     def attend(heads, first, last):
         n = len(heads)
@@ -219,11 +210,11 @@
         def group(i, carry):
             step = (i + 1) // 2
             y_ = lax.rem(y + 2 * NY + (HALF - step) * (2 * lax.rem(i, 2) - 1), NY)
-            keys = kv[0, y_].reshape(SLOTS * TILE, HD)
-            values = kv[1, y_].reshape(SLOTS * TILE, HD)
+            keys = kv[0, i].reshape(SLOTS * TILE, HD)
+            values = kv[1, i].reshape(SLOTS * TILE, HD)
             if first:
-                kv_t[0, y_] = keys.T
-                kv_t[1, y_] = values.T
+                kv_t[0, i] = keys.T
+                kv_t[1, i] = values.T
             query = q_bal[h0:h1, y_].reshape(lanes, HD)
             grad = g_in[h0:h1, y_].reshape(lanes, HD)
             scores = lax.dot_general(keys, query, nt, preferred_element_type=F32)
@@ -240,9 +231,9 @@
             weights = probs.astype(BF16)
             delta = jnp.sum(probs * dprobs, axis=0, keepdims=True)
             dscores = (probs * (dprobs - delta)).astype(BF16)
-            out_t = jnp.dot(kv_t[1, y_], weights, preferred_element_type=F32)
+            out_t = jnp.dot(kv_t[1, i], weights, preferred_element_type=F32)
             o_buf[h0:h1, y_] = out_t.T.astype(BF16).reshape(n, TILE, HD)
-            dq_t = jnp.dot(kv_t[0, y_], dscores, preferred_element_type=F32) * SCALE
+            dq_t = jnp.dot(kv_t[0, i], dscores, preferred_element_type=F32) * SCALE
             dq_bal[h0:h1, y_] = dq_t.T.astype(BF16).reshape(n, TILE, HD)
             dk = jnp.dot(dscores, query, preferred_element_type=F32).reshape(SLOTS, TILE, HD)
             dv = jnp.dot(weights, grad, preferred_element_type=F32).reshape(SLOTS, TILE, HD)
@@ -275,7 +266,24 @@
         for h in heads:
             wait(g_in.at[h], g_rs.at[h])
         if not last:
-            lax.fori_loop(0, NY, group, 0, unroll=2)
+            key_step(SLOTS - 1, 0)
+
+            def piece(part, carry):
+                @pl.when(part < PARTS - 1)
+                def _():
+                    key_step(SLOTS - 1, part + 1)
+
+                for t in range(SLOTS):
+
+                    @pl.when(z >= t)
+                    def _():
+                        wait(kv.at[0, pl.ds(part * PART, PART), t], kc_rs.at[t, part])
+
+                for i in range(PART):
+                    group(part * PART + i, carry)
+                return carry
+
+            lax.fori_loop(0, PARTS, piece, 0)
             return
 
         def some(part, carry):
@@ -349,8 +357,7 @@
     factor = jnp.where(c == 0, SCALE, 1.0).astype(F32)
 
     def read_total(y_, at):
-        d = lax.rem(y_ - y + NY, NY)
-        i = (d // HALF) * (2 * (d - HALF)) + (1 - d // HALF) * (NY - 1 - 2 * d)
+        i = turn(y_)
         total = acc[c, i, 0, at, :] + pair_in[i, 0, at, :].astype(F32) + chain_in[0, i, at, :].astype(F32)
         return total * factor
 
@@ -392,19 +399,19 @@
         wait_sent(g_in.at[h], g_ss.at[h])
         wait_sent(o_buf.at[h], o_ss.at[h])
         wait_sent(dq_buf.at[h], dq_ss.at[h])
-    for half in range(2):
-        tiles = halves[half]
+    for part in range(PARTS):
+        tiles = pl.ds(part * PART, PART)
         for t in range(SLOTS):
 
             @pl.when(z >= t)
             def _():
-                wait(kv.at[0, tiles, t], kc_ss.at[t, half])
+                wait(kv.at[0, tiles, t], kc_ss.at[t, part])
 
         for t in range(SLOTS - 1):
 
             @pl.when((z >= t) & (z < NZ - 1))
             def _():
-                wait(kv.at[0, tiles, t], kz_ss.at[t, half])
+                wait(kv.at[0, tiles, t], kz_ss.at[t, part])
 
     for part in range(PARTS):
         tiles = pl.ds(part * PART, PART)
@@ -454,7 +461,7 @@
             pltpu.VMEM((NY, *tile), BF16),
             dma, dma, dma, dma,
             dma((NH,)), dma((NH,)), dma((NH,)), dma((NH,)),
-            dma((SLOTS - 1, 2)), dma((SLOTS - 1, 2)), dma((SLOTS, 2)), dma((SLOTS, 2)),
+            dma((SLOTS - 1, PARTS)), dma((SLOTS - 1, PARTS)), dma((SLOTS, PARTS)), dma((SLOTS, PARTS)),
             dma((NH,)), dma, dma((NH,)), dma,
             dma((PARTS,)), dma((PARTS,)), dma((SLOTS - 1, PARTS, 2)), dma((SLOTS - 1, PARTS, 2)),
             dma((2,)), dma((2,)),

time: 95.5 us -> 95.9 us (level)
  no operation moved by 1% of the time
where the time goes in v5:
time: 95.9 us; the launch traced here: 95.7 us
  Pallas kernels  95.1 us (99%)
    pallas_call x1, Pallas kernels, on_device(): pl.pallas_call(kernel, out_shape=[pltpu.VMEM(a.shape, BF16) for a in (dou...  93.8 us

profile of v5, /device:TPU:1, one launch (start us, length us, event | category | flops | bytes accessed | tf_op | source)
XLA Modules:
  0.0 95.7 jit_solution(15210551345530870914)
XLA Ops:
  0.6 93.8 %shard_map.93 = (bf16[128,3072]{1,0:T(8,128)(2,1)S(1)}, bf16[128,3072]{1,0:T(8,128)(2,1)S(1)}, bf16[128,512]{1,0:T(8,128)(2,1)S(1)}, bf16[128,512]{1,0:T(8,128)(2,1)S(1)}) custom-call(s32[1,3]{1,0:T(1,128)} %bitcast.1, s32[1,8]{1,0:T(1,128)} %docs_ref.1, bf16[128,3072]{1,0:T(8,128)(2,1)} %q_ref.1, bf16[128,512]{1,0:T(8,128)(2,1)} %k_ref.1, ...), custom_call_target="tpu_custom_call" | custom-call | tf_op jit(solution)/shard_map/pallas_call | solution.py:439
  94.5 1.3 %shard_map.94 = (bf16[128,3072]{1,0:T(8,128)(2,1)}, bf16[128,3072]{1,0:T(8,128)(2,1)}, bf16[128,512]{1,0:T(8,128)(2,1)}, bf16[128,512]{1,0:T(8,128)(2,1)}) custom-call(bf16[128,3072]{1,0:T(8,128)(2,1)S(1)} %get-tuple-element.8.refs_0_, bf16[128,3072]{1,0:T(8,128)(2,1)S(1)} %get-tuple-element.9.refs_1_, bf16[128,512]{1,0:T(8,128)(2,1)S(1)} %get-tuple-element.10.refs_2_, ...), custom_call_target="tpu_custom_call" | custom-call | tf_op jit(solution)/shard_map/pallas_call | solution.py:473
